TPU v7x, 128 devices: a whole 4x4x4 slice. The times are simulated.
128 devices in a mesh: section: 2 (over core), dp: 16 (over x, y), heads: 4 (over z).
Axes of the slice: x: 4, y: 4, z: 4, core: 2. Of those that a mesh axis runs over, the one named last changes fastest.
Arguments:
- patches: bfloat16 [12544, 768], P('dp'), may hold values from -6 to 6
- mask_flags: int32 [64, 196], P('dp'), may hold values 0 or 1
- image_tags: int32 [64], P('dp'), may hold values from 0 to 7
- mask_token: float32 [768], replicated, may hold values from -6 to 6
- group_table: float32 [8, 768], replicated, may hold values from -3 to 3
- qkv_weight: float32 [2, 768, 3, 768], P('section', 'dp'), may hold values from -0.21875 to 0.21875
- query_value_bias: float32 [2, 2, 768], P('section'), may hold values from -3 to 3
- out_weight: float32 [2, 768, 768], P('section', None, 'dp'), may hold values from -0.625 to 0.625
- up_weight: float32 [2, 768, 3072], P('section', 'dp'), may hold values from -0.21875 to 0.21875
- hidden_bias: float32 [2, 3072], P('section'), may hold values from -3 to 3
- down_weight: float32 [2, 3072, 768], P('section', None, 'dp'), may hold values from -0.109375 to 0.109375
- norm_gains: float32 [2, 2, 768], P('section'), may hold values from 0.5 to 1.5
- norm_biases: float32 [2, 4, 768], P('section'), may hold values from -2 to 2
- cotangent: bfloat16 [12544, 768], P('dp'), may hold values from -6 to 6
Outputs:
- stream_ends: float32 [2, 12544, 768], P('section', 'dp')
- grad_qkv: float32 [2, 768, 3, 768], P('section', 'dp')
- grad_qv_bias: float32 [2, 2, 768], P('section')
- grad_out: float32 [2, 768, 768], P('section', None, 'dp')
- grad_up: float32 [2, 768, 3072], P('section', 'dp')
- grad_hidden_bias: float32 [2, 3072], P('section')
- grad_down: float32 [2, 3072, 768], P('section', None, 'dp')
- grad_gains: float32 [2, 2, 768], P('section')
- grad_biases: float32 [2, 4, 768], P('section')
- grad_token: float32 [768], P('section')
- grad_table: float32 [8, 768], P(None, 'section')
Inputs may be any that keep to these rules, and one draw needn't show every extreme that they name: `image_tags`: the dataset group of each image; micro-batch (group mod 2) sizes may differ from device to device. `mask_flags`: 1 marks a masked patch.
All inputs are finite; a program needn't handle non-finite values. No bound on the sum of `mask_flags` on one device may be relied on, other than what follows from the above.
Results may differ from a plain program's by a relative error of at most 0.013.
Values may be sent and summed in bfloat16 or wider, within the bound.
No kernel may reach another device: no remote copies, remote signals or barrier semaphores. Data moves between devices by JAX's collectives and lax.ppermute only.
A program may use at most 192 MiB of HBM per device.

v0:
```python
import functools

import jax
import jax.numpy as jnp
from jax import lax
from jax.experimental import pallas as pl
from jax.experimental.pallas import tpu as pltpu
from jax.sharding import PartitionSpec as P

D = 768
HD = 64
FF = 3072
PATCHES = 196
ROWS = 208
GROUPS = 8
HALF = D // 2
HALF_FF = FF // 2
PAIR = 2 * HD
STEPS = 3
CHUNK = HALF_FF // STEPS
FEED = 2 * HALF_FF
ATTN = 4 * HALF
LAYER = FEED + ATTN
JOINED = LAYER + FEED
SIDE = 4
BLOCK = D // SIDE**2
MESH = ("section", "dp", "heads")
SWAP = [(0, 1), (1, 0)]
LIMIT = 48 * 2**20
SCALE = HD ** (-0.5)
epsilon = 1e-06
f32 = jnp.float32
low = jnp.bfloat16


def dot(left, right):
    return jnp.dot(left, right, preferred_element_type=f32)


def dot_t(left, right):
    return lax.dot_general(left, right, (((1,), (1,)), ((), ())), preferred_element_type=f32)


def t_dot(left, right):
    return lax.dot_general(left, right, (((0,), (0,)), ((), ())), preferred_element_type=f32)


def both(own, other):
    return own[...].astype(f32) + other[...].astype(f32)


def column_sum(value):
    return jnp.sum(value.astype(f32), axis=0, keepdims=True)


def stats(value):
    average = jnp.mean(value, axis=-1, keepdims=True)
    centred = value - average
    rate = lax.rsqrt(jnp.mean(centred * centred, axis=-1, keepdims=True) + epsilon)
    return centred * rate, rate


def norm_back(value, gain, grad):
    x, rate = stats(value)
    scaled = grad * gain
    inner = scaled - jnp.mean(scaled, axis=-1, keepdims=True)
    inner = inner - x * jnp.mean(scaled * x, axis=-1, keepdims=True)
    return rate * inner, column_sum(grad * x), column_sum(grad)


def gauss(value):
    return 0.5 + 0.5 * lax.erf(value * 0.7071067811865476), jnp.exp(value * value * -0.5) * 0.3989422804014327


def head_masks():
    left = lax.broadcasted_iota(jnp.int32, (ROWS, PAIR), 1) < HD
    nothing = jnp.zeros((ROWS, PAIR), low)
    return left, (lambda rows: jnp.where(left, rows, nothing), lambda rows: jnp.where(left, nothing, rows))


def raw_scores(key_rows, queries):
    scores = dot_t(key_rows, queries) * SCALE
    return jnp.where(lax.broadcasted_iota(jnp.int32, scores.shape, 0) < PATCHES, scores, -1e30)


def accumulate(step, total, part, low_out):
    @pl.when(step == 0)
    def _():
        total[...] = part

    @pl.when(step > 0)
    def _():
        total[...] += part

    @pl.when(step == STEPS - 1)
    def _():
        low_out[...] = total[...].astype(low)


def slot_rows(slots):
    for i in range(SIDE):
        for j in range(SIDE):
            yield i, j, pl.multiple_of(slots[i] * (SIDE * BLOCK) + slots[SIDE + j] * BLOCK, 16)


def place_rows(slots, pieces, weight, width):
    for i, j, row in slot_rows(slots):
        weight[pl.ds(row, BLOCK), :width] = pieces[j // 2][j % 2, i]
        weight[pl.ds(row, BLOCK), width:] = pieces[2 + i // 2][i % 2, j]


def send_rows(slots, grads, blocks, width):
    for i, j, row in slot_rows(slots):
        blocks[i // 2][i % 2, j] = grads[pl.ds(row, BLOCK), :width]
        blocks[2 + j // 2][j % 2, i] = grads[pl.ds(row, BLOCK), width:]


def attention_kernel(second, *refs):
    if second:
        base, own, other, last_bias, norms, offset, weight, stream_out, *refs = refs
    else:
        slots, base, norms, offset, *refs = refs
        pieces, (weight, *refs) = refs[:SIDE], refs[SIDE:]
    normed_out, packed_out, lse_out, context_out, part_out, total = refs
    step = pl.program_id(0)

    @pl.when(step == 0)
    def _():
        stream = base[...]
        if second:
            stream = (stream + (both(own, other) + last_bias[...])).astype(low).astype(f32)
            stream_out[...] = stream
        normed_out[...] = (stats(stream)[0] * norms[0:1] + norms[2:3]).astype(low)

    if not second:
        place_rows(slots, pieces, weight, 2 * PAIR)
    packed = (dot(normed_out[...], weight[:, : 3 * PAIR]) + offset[...]).astype(low)
    packed_out[...] = packed
    left, choose = head_masks()
    queries, keys, values = (packed[:, k * PAIR : (k + 1) * PAIR] for k in range(3))
    found = []
    for head in range(2):
        scores = raw_scores(keys, choose[head](queries))
        summit = jnp.max(scores, axis=0, keepdims=True)
        raised = jnp.exp(scores - summit)
        whole = jnp.sum(raised, axis=0, keepdims=True)
        lse_out[0, head : head + 1, :] = summit + jnp.log(whole)
        found.append(t_dot((raised * (1.0 / whole)).astype(low), values))
    context = jnp.where(left, found[0], found[1]).astype(low)
    context_out[...] = context
    accumulate(step, total, dot_t(context, weight[:, 3 * PAIR :]), part_out)


def forward_kernel(stream, own, other, norms, bias, weight, middle_out, normed_out, upper_out, part_out, total):
    step = pl.program_id(0)

    @pl.when(step == 0)
    def _():
        middle = stream[...] + (both(own, other) + norms[3:4])
        middle_out[...] = middle
        normed_out[...] = (stats(middle)[0] * norms[1:2] + norms[4:5]).astype(low)

    upper = dot(normed_out[...], weight[:, :CHUNK]) + bias[...]
    upper_out[...] = upper
    hidden = (upper * gauss(upper)[0]).astype(low)
    accumulate(step, total, dot_t(hidden, weight[:, CHUNK:]), part_out)


def turn_kernel(
    branch, stream, own, other, norms, bias, weight,
    grads_out, middle_out, mixed_out, part_out, bias_out, rows_out, normed, mixed, total,
):
    step = pl.program_id(0)

    @pl.when(step == 0)
    def _():
        middle = stream[...] + (both(own, other) + norms[3:4])
        middle_out[...] = middle
        normed[...] = (stats(middle)[0] * norms[1:2] + norms[4:5]).astype(low)
        rows_out[2:3] = column_sum(branch[...])

    rows = branch[...]
    upper = dot(normed[...], weight[:, :CHUNK]) + bias[...]
    share, density = gauss(upper)
    hidden = (upper * share).astype(low)
    grad_upper = (dot(rows, weight[:, CHUNK:]) * (share + upper * density)).astype(low)
    accumulate(step, total, dot_t(grad_upper, weight[:, :CHUNK]), part_out)
    grads_out[:, :CHUNK] = t_dot(normed[...], grad_upper).astype(low)
    grads_out[:, CHUNK:] = t_dot(rows, hidden).astype(low)
    bias_out[...] = column_sum(grad_upper)
    accumulate(step, mixed, dot_t(hidden, weight[:, CHUNK:]), mixed_out)


def backward_kernel(
    grad, own, other, stream, gains, normed, upper, weight, _, grads, part_out, bias_out, rows_out, branch, total
):
    step = pl.program_id(0)

    @pl.when(step == 0)
    def _():
        into, gain, shift = norm_back(stream[...], gains[0:1], both(own, other))
        branch[...] = (grad[...] + into).astype(low)
        rows_out[0:1] = gain
        rows_out[1:2] = shift
        rows_out[2:3] = column_sum(branch[...])

    rows = branch[...]
    upper_now = upper[...]
    share, density = gauss(upper_now)
    hidden = (upper_now * share).astype(low)
    grad_upper = (dot(rows, weight[:, CHUNK:]) * (share + upper_now * density)).astype(low)
    accumulate(step, total, dot_t(grad_upper, weight[:, :CHUNK]), part_out)
    grads[:, :CHUNK] = t_dot(normed[...], grad_upper).astype(low)
    grads[:, CHUNK:] = t_dot(rows, hidden).astype(low)
    bias_out[...] = column_sum(grad_upper)


def attention_back_kernel(second, *refs):
    if not second:
        slots, *refs = refs
    branch, own, other, middle, norms, normed, packed, lse, context, weight, *refs = refs
    if second:
        _, grads, *refs = refs
    else:
        blocks, refs = refs[:SIDE], refs[SIDE:]
    middle_out, part_out, rows_out, packed_out, attn, total, grad_packed, *refs = refs
    if not second:
        (grads,) = refs
    step = pl.program_id(0)

    @pl.when(step == 0)
    def _():
        into, gain, shift = norm_back(middle[...], norms[1:2], both(own, other))
        grad_middle = branch[...].astype(f32) + into
        middle_out[...] = grad_middle
        attn[...] = grad_middle.astype(low)
        rows_out[0:1] = gain
        rows_out[1:2] = shift
        rows_out[2:3] = column_sum(attn[...])

    grad_pair = dot(attn[...], weight[:, 3 * PAIR :]).astype(low)
    left, choose = head_masks()
    queries, keys, values = (packed[:, k * PAIR : (k + 1) * PAIR] for k in range(3))
    found = []
    for head in range(2):
        soft = jnp.exp(raw_scores(keys, choose[head](queries)) - lse[0, head : head + 1, :])
        grad_probs = dot_t(values, choose[head](grad_pair))
        within = jnp.sum(grad_probs * soft, axis=0, keepdims=True)
        grad_scores = (soft * (grad_probs - within)).astype(low)
        found.append((t_dot(grad_scores, keys) * SCALE, dot(grad_scores, queries) * SCALE, dot(soft.astype(low), grad_pair)))
    for k in range(3):
        grad_packed[:, k * PAIR : (k + 1) * PAIR] = jnp.where(left, found[0][k], found[1][k]).astype(low)
    rows = grad_packed[...]
    accumulate(step, total, dot_t(rows, weight[:, : 3 * PAIR]), part_out)
    grads[:, : 3 * PAIR] = t_dot(normed[...], rows).astype(low)
    grads[:, 3 * PAIR :] = t_dot(attn[...], context[...]).astype(low)
    if not second:
        send_rows(slots, grads, blocks, 2 * PAIR)
    packed_out[...] = column_sum(rows)


def last_kernel(
    core, grad_middle, own, other, stream, norms, masked, tag, middle, mixed, mixed_other, last_bias,
    rows_one, sums_one, turn_rows, bias_one, rows_zero, sums_zero, back_rows, bias_zero, rows_out, vectors_out,
):
    into, gain, shift = norm_back(stream[...], norms[0:1], both(own, other))
    grad_zero = grad_middle[...] + into
    hidden = masked[...] > 0.5
    final = middle[...] + (both(mixed, mixed_other) + last_bias[...])
    first = core[0] == 0
    rows_out[...] = jnp.where(first, jnp.where(hidden, 0.0, grad_zero), final).astype(low)
    for at, gain_one, shift_one, attn_rows, feed_rows, sums, bias in (
        (0, gain, shift, rows_zero, back_rows, sums_zero, bias_zero),
        (9, back_rows[0:1], back_rows[1:2], rows_one, turn_rows, sums_one, bias_one),
    ):
        for k, row in enumerate((gain_one, attn_rows[0:1], shift_one, attn_rows[2:3], attn_rows[1:2], feed_rows[2:3])):
            vectors_out[at + k : at + k + 1] = row
        for k in range(STEPS):
            for part in range(2):
                to = part * HALF + k * PAIR
                vectors_out[at + 6 : at + 7, to : to + PAIR] = sums[:, (3 * k + 2 * part) * PAIR : (3 * k + 2 * part + 1) * PAIR]
        for k in range(2):
            vectors_out[at + 7 + k : at + 8 + k] = bias[:, k * D : (k + 1) * D]
    vectors_out[18:19] = column_sum(jnp.where(hidden, grad_zero, 0.0))
    table = column_sum(grad_zero)
    for group in range(GROUPS):
        vectors_out[19 + group : 20 + group] = jnp.where(tag[0] == group, table, 0.0)
    vectors_out[27:32] = jnp.zeros((5, D), f32)


def ends_kernel(order, parts, out):
    for k in range(SIDE):
        out[k * PATCHES : (k + 1) * PATCHES] = parts[order[k]].astype(f32)[:PATCHES]


def shards_kernel(core, qkv, out, up, down, mine_out, sent_out):
    def fill(half, target):
        for k in range(STEPS):
            at = slice(half * HALF_FF + k * CHUNK, half * HALF_FF + (k + 1) * CHUNK)
            target[:, 2 * k * CHUNK : (2 * k + 1) * CHUNK] = up[:, at].astype(low)
            target[:, (2 * k + 1) * CHUNK : (2 * k + 2) * CHUNK] = down[:, at].astype(low)
            at = slice(half * HALF + k * PAIR, half * HALF + (k + 1) * PAIR)
            for part, rows in enumerate((qkv[0, :, at], qkv[1, :, at], qkv[2, :, at], out[:, at])):
                to = FEED + (part // 2) * 2 * HALF + (2 * k + part % 2) * PAIR
                target[:, to : to + PAIR] = rows.astype(low)

    for index in range(2):
        @pl.when(core[0] == index)
        def _():
            fill(index, mine_out)
            fill(1 - index, sent_out)


def grads_kernel(first_half, second_half, qkv_out, out_out, up_out, down_out):
    for h, part in enumerate((first_half, second_half)):
        for k in range(STEPS):
            to = slice(h * HALF_FF + k * CHUNK, h * HALF_FF + (k + 1) * CHUNK)
            up_out[:, to] = part[:, 2 * k * CHUNK : (2 * k + 1) * CHUNK].astype(f32)
            down_out[:, to] = part[:, (2 * k + 1) * CHUNK : (2 * k + 2) * CHUNK].astype(f32)
            to = slice(h * HALF + k * PAIR, h * HALF + (k + 1) * PAIR)
            at = FEED + 4 * k * PAIR
            for c in range(3):
                qkv_out[c, :, to] = part[:, at + c * PAIR : at + (c + 1) * PAIR].astype(f32)
            out_out[:, to] = part[:, at + 3 * PAIR : at + 4 * PAIR].astype(f32)


def whole(array):
    return pl.BlockSpec(array.shape, lambda *_: (0,) * len(array.shape))


def shaped(shape, kind=f32):
    return jax.ShapeDtypeStruct(shape, kind)


def call(kernel, name, operands, outs, specs, flops=0, moved=2**20, grid=STEPS, alias=None, scratch=()):
    def spec(key, array):
        return specs.get(key) or whole(array)

    return pl.pallas_call(
        kernel,
        name=name,
        grid=(grid,),
        in_specs=[spec(("in", k), a) for k, a in enumerate(operands)],
        out_specs=[spec(("out", k), a) for k, a in enumerate(outs)],
        out_shape=outs,
        scratch_shapes=scratch,
        input_output_aliases=alias or {},
        cost_estimate=pl.CostEstimate(flops=flops, bytes_accessed=moved, transcendentals=0),
        compiler_params=pltpu.CompilerParams(vmem_limit_bytes=LIMIT),
    )(*operands)


SMALL = pl.BlockSpec(memory_space=pltpu.SMEM)
LEFT = pl.BlockSpec(memory_space=pl.ANY)


def by_step(shape, start=0):
    return pl.BlockSpec(shape, lambda i: (0,) * (len(shape) - 1) + (start + i,))


FEED_WEIGHT = by_step((D, 2 * CHUNK))
ATTN_WEIGHT = by_step((D, 4 * PAIR))
ATTN_JOINED = by_step((D, 4 * PAIR), 2 * FEED // (4 * PAIR))
FEED_ZERO = by_step((D, 2 * CHUNK), STEPS)
ATTN_PIECE = by_step((2, SIDE, BLOCK, 2 * PAIR))
TRIPLE = by_step((ROWS, 3 * PAIR))
LSE = pl.BlockSpec((1, 8, ROWS), lambda i: (i, 0, 0))
STREAM = shaped((ROWS, D))
STREAM_LOW = shaped((ROWS, D), low)
TOTAL = pltpu.VMEM((ROWS, D), f32)
ATTN_FLOPS = 2 * ROWS * D * ATTN
FEED_FLOPS = 2 * ROWS * D * FEED
HEAD_FLOPS = 2 * ROWS * ROWS * PAIR * 2 * STEPS


def attention_call(layer, entry, norms, offset, weights):
    second = layer == 1
    operands = (*entry, norms, offset, *weights)
    outs = [STREAM_LOW, shaped((ROWS, 3 * HALF), low), shaped((STEPS, 8, ROWS)), shaped((ROWS, HALF), low), STREAM_LOW]
    outs = [STREAM if second else shaped((D, ATTN), low), *outs]
    last = len(operands) - 1
    specs = {("out", 2): TRIPLE, ("out", 3): LSE, ("out", 4): by_step((ROWS, PAIR))}
    if second:
        specs["in", last] = ATTN_JOINED
        specs["in", last - 1] = by_step((1, 3 * PAIR))
    else:
        specs["in", 0] = SMALL
        specs["out", 0] = ATTN_WEIGHT
        specs["in", last - SIDE] = by_step((1, 3 * PAIR))
        for k in range(SIDE):
            specs["in", last - k] = ATTN_PIECE
    return call(
        functools.partial(attention_kernel, second), f"attention_{layer}", operands, outs, specs,
        ATTN_FLOPS + 2 * HEAD_FLOPS, 8 * D * ATTN, scratch=[TOTAL],
    )


def forward_call(stream, part, part_other, norms, bias_up, weight):
    return call(
        forward_kernel, "feed_0", (stream, part, part_other, norms, bias_up, weight),
        [STREAM, STREAM_LOW, shaped((ROWS, HALF_FF)), STREAM_LOW],
        {("in", 4): by_step((1, CHUNK)), ("in", 5): FEED_ZERO, ("out", 2): by_step((ROWS, CHUNK))},
        FEED_FLOPS, 6 * D * FEED, scratch=[TOTAL],
    )


def turn_call(branch, stream, part, part_other, norms, bias_up, weight):
    return call(
        turn_kernel, "feed_1", (branch, stream, part, part_other, norms, bias_up, weight),
        [shaped((D, JOINED), low), STREAM, STREAM_LOW, STREAM_LOW, shaped((1, HALF_FF)), shaped((8, D))],
        {("in", 5): by_step((1, CHUNK)), ("in", 6): FEED_WEIGHT, ("out", 0): FEED_WEIGHT, ("out", 4): by_step((1, CHUNK))},
        3 * FEED_FLOPS, 8 * D * FEED, scratch=[pltpu.VMEM((ROWS, D), low), TOTAL, TOTAL],
    )


def backward_call(entry, normed, upper, weight, grads):
    return call(
        backward_kernel, "feed_back_0", (*entry, normed, upper, weight, grads),
        [shaped((D, JOINED), low), STREAM_LOW, shaped((1, HALF_FF)), shaped((8, D)), STREAM_LOW],
        {
            ("in", 6): by_step((ROWS, CHUNK)), ("in", 7): FEED_ZERO, ("in", 8): LEFT,
            ("out", 0): FEED_ZERO, ("out", 2): by_step((1, CHUNK)),
        },
        2 * FEED_FLOPS, 8 * D * FEED, alias={8: 0}, scratch=[TOTAL],
    )


def attention_back_call(layer, entry, branch, part, part_other, middle, norms, normed, packed, lse, context, weight, grads):
    second = layer == 1
    operands = (*entry, branch, part, part_other, middle, norms, normed, packed, lse, context, weight, *grads)
    outs = [shaped((D, JOINED), low)] if second else [shaped((2, SIDE, BLOCK, 2 * HALF), low)] * SIDE
    skip, count = len(entry), len(outs)
    specs = {
        ("in", skip + 6): TRIPLE, ("in", skip + 7): LSE, ("in", skip + 8): by_step((ROWS, PAIR)),
        ("in", skip + 9): ATTN_JOINED if second else ATTN_WEIGHT, ("out", count + 3): by_step((1, 3 * PAIR)),
    }
    scratch = [pltpu.VMEM((ROWS, D), low), TOTAL, pltpu.VMEM((ROWS, 3 * PAIR), low)]
    if second:
        specs["in", 10], specs["out", 0] = LEFT, ATTN_JOINED
    else:
        specs["in", 0] = SMALL
        for k in range(SIDE):
            specs["out", k] = ATTN_PIECE
        scratch.append(pltpu.VMEM((D, 4 * PAIR), low))
    made = call(
        functools.partial(attention_back_kernel, second), f"attention_back_{layer}", operands,
        [*outs, STREAM, STREAM_LOW, shaped((8, D)), shaped((1, 3 * HALF))], specs,
        2 * ATTN_FLOPS + 5 * HEAD_FLOPS, 8 * D * ATTN, alias={10: 0} if second else None, scratch=scratch,
    )
    return made[:count], made[count:]


def swap(value):
    return lax.ppermute(value, "section", SWAP)


def routes(axis, turn):
    pairs = []
    for place in range(2 * SIDE**3):
        spot = [place // SIDE**3, place // SIDE**2 % SIDE, place // SIDE % SIDE, place % SIDE]
        spot[axis + 1] ^= 1 if spot[0] == turn else 3
        pairs.append((place, ((spot[0] * SIDE + spot[1]) * SIDE + spot[2]) * SIDE + spot[3]))
    return pairs


def trade(value, axis, turn):
    return lax.ppermute(value, MESH, routes(axis, turn))


def add(*values):
    return functools.reduce(jnp.add, (v.astype(f32) for v in values)).astype(low)


def both_of(own, axis, turn):
    return jnp.stack([own, trade(own, axis, turn)])


def gather_first(own, axis):
    pair = both_of(own, axis, 0)
    return jnp.concatenate([pair, trade(pair, axis, 1)])


def gather_second(own, axis):
    pair = both_of(own, axis, 0)
    return pair, trade(pair, axis, 1)


def halves_of(kept, got):
    middle = kept.shape[0] // 2
    return add(kept[:middle], got[:middle]), add(kept[middle:], got[middle:])


def all_sum(value, axis):
    value = value + trade(value, axis, 0)
    return value + trade(value, axis, 1)


tied = lax.optimization_barrier


def per_device(
    patches, mask_flags, image_tags, mask_token, group_table, qkv_weight, query_value_bias, out_weight,
    up_weight, hidden_bias, down_weight, norm_gains, norm_biases, cotangent,
):
    place = lax.axis_index("heads")
    core = lax.axis_index("section")
    first = core == 0

    rows = qkv_weight.shape[1]
    mine, other = call(
        shards_kernel, "shards",
        (core.reshape(1), qkv_weight[0].transpose(1, 0, 2), out_weight[0].T, up_weight[0], down_weight[0].T),
        [shaped((rows, LAYER), low)] * 2, {("in", 0): SMALL}, grid=1,
    )
    other = swap(other)
    zero, one = jnp.where(first, mine, other), jnp.where(first, other, mine)

    def by_pair(wide):
        return [wide[:, s * 2 * HALF + k * 2 * PAIR : s * 2 * HALF + (k + 1) * 2 * PAIR] for k in range(STEPS) for s in (0, 1)]

    shard = jnp.concatenate([one[:, :FEED], zero[:, :FEED], *by_pair(one[:, FEED:])], axis=1)
    weights = lax.all_gather(shard, "dp", axis=0, tiled=True)
    pieces = gather_first(zero[:, FEED : FEED + 2 * HALF], 0), gather_first(zero[:, FEED + 2 * HALF :], 1)
    pieces = (*gather_second(pieces[0], 1), *gather_second(pieces[1], 0))
    later = (patches, mask_flags, image_tags, mask_token, group_table, cotangent, norm_gains, norm_biases, query_value_bias, hidden_bias)
    later, _ = tied((later, shard))
    patches, mask_flags, image_tags, mask_token, group_table, cotangent, norm_gains, norm_biases, query_value_bias, hidden_bias = later

    x, y = lax.axis_index("dp") // SIDE, lax.axis_index("dp") % SIDE
    flips = jnp.where(first, jnp.array([0, 1, 3, 2], jnp.int32), jnp.array([0, 3, 1, 2], jnp.int32))
    slots = jnp.concatenate([x ^ flips, y ^ flips])
    order = jnp.argmax((place ^ flips)[None, :] == jnp.arange(SIDE, dtype=jnp.int32)[:, None], axis=1).astype(jnp.int32)

    def half_of(vector):
        return jnp.where(first, vector[..., : vector.shape[-1] // 2], vector[..., vector.shape[-1] // 2 :])

    vectors = lax.all_gather(
        jnp.concatenate([norm_gains[0], norm_biases[0], query_value_bias[0], hidden_bias[0].reshape(4, D)]),
        "section", axis=0,
    )
    norms, offsets, bias_ups = [], [], []
    for layer in range(2):
        v = vectors[layer]
        norms.append(jnp.pad(v[:6], ((0, 2), (0, 0))))
        query, value = half_of(v[6:8]).reshape(2, STEPS, PAIR)
        offsets.append(jnp.stack([query, jnp.zeros_like(query), value], axis=1).reshape(1, 3 * HALF))
        bias_ups.append(half_of(v[8:12].reshape(1, FF)))

    def own(rows_of):
        return lax.dynamic_slice_in_dim(rows_of, place * PATCHES, PATCHES, 0)

    def padded(value):
        return jnp.pad(value, ((0, ROWS - PATCHES), (0, 0)))

    masked = lax.dynamic_slice_in_dim(mask_flags, place, 1, 0).reshape(PATCHES, 1).astype(f32)
    tag = lax.dynamic_slice_in_dim(image_tags, place, 1, 0)
    onehot = (tag[:, None] == jnp.arange(GROUPS, dtype=jnp.int32)[None, :]).astype(f32)
    image_row = jnp.sum(onehot.T * group_table, axis=0, keepdims=True)
    stream_zero = padded(jnp.where(masked > 0, mask_token[None, :], own(patches).astype(f32)) + image_row)
    seed, masked = padded(own(cotangent)), padded(masked)

    attn_zero, normed, packed, lse, context, part = attention_call(0, (slots, stream_zero), norms[0], offsets[0], pieces)
    middle, normed_two, upper, mixed = forward_call(stream_zero, part, swap(part), norms[0], bias_ups[0], weights)
    kept = (middle, norms[0], normed, packed, lse, context, attn_zero)
    stream_one, normed, packed, lse, context, part = attention_call(
        1, (middle, mixed, swap(mixed), norms[0][5:6]), norms[1], offsets[1], [weights]
    )
    grads, middle, mixed, part, bias_one, turn_rows = turn_call(
        seed, stream_one, part, swap(part), norms[1], bias_ups[1], weights
    )
    (grads,), (grad_middle, part, rows_one, sums_one) = attention_back_call(
        1, (), seed, part, swap(part), middle, norms[1], normed, packed, lse, context, weights, [grads]
    )
    grads, part, bias_zero, back_rows, branch = backward_call(
        (grad_middle, part, swap(part), stream_one, norms[1]), normed_two, upper, weights, grads
    )
    joined = lax.psum_scatter(grads, "dp", scatter_dimension=0, tiled=True)
    (zero, sent, zero_too, sent_too), (grad_middle, part, rows_zero, sums_zero) = attention_back_call(
        0, (slots,), branch, part, swap(part), *kept, []
    )
    rows_out, small = call(
        last_kernel, "last",
        (
            core.reshape(1), grad_middle, part, swap(part), stream_zero, norms[0], masked, tag, middle, mixed, swap(mixed),
            norms[1][5:6], rows_one, sums_one, turn_rows, bias_one, rows_zero, sums_zero, back_rows, bias_zero,
        ),
        [STREAM_LOW, shaped((32, D))], {("in", 0): SMALL, ("in", 7): SMALL}, grid=1,
    )

    got, got_too = trade(sent, 0, 1), trade(sent_too, 1, 1)
    (zero, sent), (zero_too, sent_too) = halves_of(zero, got), halves_of(zero_too, got_too)
    got, got_too = trade(sent, 0, 0), trade(sent_too, 1, 0)
    (zero, sent), (zero_too, sent_too) = halves_of(zero[0], got[0]), halves_of(zero_too[0], got_too[0])
    got, got_too = trade(sent, 1, 1), trade(sent_too, 0, 1)
    (zero, sent), (zero_too, sent_too) = halves_of(zero, got), halves_of(zero_too, got_too)
    got, got_too = trade(sent, 1, 0), trade(sent_too, 0, 0)
    attn_sum = jnp.concatenate(by_pair(jnp.concatenate([add(zero[0], got[0]), add(zero_too[0], got_too[0])], axis=1)), axis=1)

    def z_sum(value):
        value = add(value, trade(value, 2, 0))
        return add(value, trade(value, 2, 1))

    attn_sum = z_sum(attn_sum)
    for axis in range(3):
        small = all_sum(small, axis)
    ends = both_of(rows_out, 2, 0)
    ends = jnp.concatenate([ends, trade(ends, 2, 1)])
    (ends_here,) = call(
        ends_kernel, "ends", (order, ends), [shaped((SIDE * PATCHES, D))], {("in", 0): SMALL}, grid=1
    )
    small_mine = jnp.where(first, small[:9], small[9:18])
    half_other = swap(jnp.where(first, small[15:18], small[6:9]))
    half_mine = small_mine[6:9]
    half_both = jnp.where(first, half_mine, half_other), jnp.where(first, half_other, half_mine)
    grad_qv = jnp.concatenate([h[0].reshape(2, HALF) for h in half_both], axis=1)
    grad_hidden = jnp.concatenate([h[1:].reshape(1, HALF_FF) for h in half_both], axis=1)
    ends_grads = half_of(small[18:27])

    joined, attn_sum, ends_here, small_mine, grad_qv, grad_hidden, ends_grads = tied(
        (joined, attn_sum, ends_here, small_mine, grad_qv, grad_hidden, ends_grads)
    )
    joined = z_sum(joined)
    zero = jnp.concatenate([joined[:, FEED : 2 * FEED], attn_sum], axis=1)
    one = jnp.concatenate([joined[:, :FEED], joined[:, 2 * FEED :]], axis=1)
    mine = jnp.where(first, zero, one)
    other = swap(jnp.where(first, one, zero))
    grad_qkv, grad_out, grad_up, grad_down = call(
        grads_kernel, "grads", (jnp.where(first, mine, other), jnp.where(first, other, mine)),
        [shaped((3, rows, D)), shaped((rows, D)), shaped((rows, FF)), shaped((rows, FF))], {}, grid=1,
    )
    return (
        ends_here[None], grad_qkv.transpose(1, 0, 2)[None], grad_qv[None], grad_out.T[None], grad_up[None], grad_hidden, grad_down.T[None],
        small_mine[None, 0:2], small_mine[None, 2:6], ends_grads[0], ends_grads[1:],
    )


def solution(mesh):
    in_specs = (
        P("dp", None), P("dp", None), P("dp"), P(), P(),
        P("section", "dp", None, None), P("section", None, None), P("section", None, "dp"),
        P("section", "dp", None), P("section", None), P("section", None, "dp"),
        P("section", None, None), P("section", None, None), P("dp", None),
    )
    out_specs = (
        P("section", "dp", None), P("section", "dp", None, None), P("section", None, None),
        P("section", None, "dp"), P("section", "dp", None), P("section", None), P("section", None, "dp"),
        P("section", None, None), P("section", None, None), P("section"), P(None, "section"),
    )
    return jax.shard_map(per_device, mesh=mesh, in_specs=in_specs, out_specs=out_specs, check_vma=False)
```

profile of v0, /device:TPU:1, one launch (start us, length us, event | category | flops | bytes accessed | tf_op | source)
XLA Modules:
  0.0 293.4 jit_solution(10955871269447869959)
XLA Ops:
  17.1 2.9 collective-permute-start.5
  20.0 2.5 collective-permute-start.1
  25.4 3.2 %collective-permute-done.6 = bf16[2,48,768]{2,1,0:T(8,128)(2,1)S(1)} collective-permute-done((bf16[2,48,768]{2,1,0:T(8,128)(2,1)S(1)}, bf16[2,48,768]{2,1,0:T(8,128)(2,1)S(1)}, u32[]{:S(2)}, u32[]{:S(2)}) %collective-permute-start.6) | collective-permute-done | bytes 147488 | tf_op jit(solution)/shard_map/ppermute | solution.py:467
  29.0 2.3 collective-permute-start.3
  31.4 10.7 %collective-permute-done.7 = bf16[4,48,768]{2,1,0:T(8,128)(2,1)S(1)} collective-permute-done((bf16[4,48,768]{2,1,0:T(8,128)(2,1)S(1)}, bf16[4,48,768]{2,1,0:T(8,128)(2,1)S(1)}, u32[]{:S(2)}, u32[]{:S(2)}) %collective-permute-start.7) | collective-permute-done | bytes 294944 | tf_op jit(solution)/shard_map/ppermute | solution.py:467
  44.9 7.7 %collective-permute-done.8.refs_7_ = bf16[2,4,48,768]{3,2,1,0:T(8,128)(2,1)} collective-permute-done((bf16[2,4,48,768]{3,2,1,0:T(8,128)(2,1)S(1)}, bf16[2,4,48,768]{3,2,1,0:T(8,128)(2,1)}, u32[]{:S(2)}, u32[]{:S(2)}) %collective-permute-start.8) | collective-permute-done | bytes 589856 | tf_op jit(solution)/shard_map/ppermute | solution.py:467
  54.1 5.9 %attention_0.1 = (bf16[768,1536]{1,0:T(8,128)(2,1)}, bf16[208,768]{1,0:T(8,128)(2,1)S(1)}, bf16[208,1152]{1,0:T(8,128)(2,1)S(1)}, f32[3,8,208]{2,1,0:T(8,128)S(1...) custom-call(s32[8]{0:T(128)S(1)} %pad_add_fusion.refs_0_, f32[208,768]{1,0:T(8,128)S(1)} %pad.20.refs_1_.stream, ...), custom_call_target="tpu_custom_call" | custom-call | flops 623640576 | bytes 9437184 | tf_op jit(solution)/shard_map/attention_0/pallas_call | solution.py:339
  61.5 4.6 %collective-permute-start.9 = (bf16[208,768]{1,0:T(8,128)(2,1)S(1)}, bf16[208,768]{1,0:T(8,128)(2,1)S(1)}, u32[]{:S(2)}, u32[]{:S(2)}) collective-permute-start(bf16[208,768]{1,0:T(8,128)(2,1)S(1)} %get-tuple-element.89.own), channel_id=1, source_target_pairs={{0,64},{64,0},{1,65},{65,1},{2,66},{66,2},{3,67},{67,3},{4,68},{68... | collective-permute-start | bytes 958472 | tf_op jit(solution)/shard_map/ppermute | solution.py:454
  67.3 41.1 %all-gather.4.cloned.1.call-done.weight.refs_6_.refs_9_ = bf16[768,7680]{1,0:T(8,128)(2,1)} async-done(((bf16[48,7680]{1,0:T(8,128)(2,1)}), bf16[768,7680]{1,0:T(8,128)(2,1)}) %all-gather.4.cloned.1.call-update) | async-done | bytes 11796496 | tf_op jit(solution)/shard_map/all_gather | solution.py:522
  109.4 4.7 %feed_0.1 = (f32[208,768]{1,0:T(8,128)S(1)}, bf16[208,768]{1,0:T(8,128)(2,1)S(1)}, f32[208,1536]{1,0:T(8,128)S(1)}, bf16[208,768]{1,0:T(8,128)(2,1)S(1)}) custom-call(f32[208,768]{1,0:T(8,128)S(1)} %pad.20.refs_1_.stream, bf16[208,768]{1,0:T(8,128)(2,1)S(1)} %copy-done.17, bf16[208,768]{1,0:T(8,128)(2,1)S(1)} %collective-permute-done.9.other, ...), custom_call_target="tpu_custom_call" | custom-call | flops 981467136 | bytes 14155776 | tf_op jit(solution)/shard_map/feed_0/pallas_call | solution.py:339
  116.1 4.9 %attention_1.1 = (f32[208,768]{1,0:T(8,128)S(1)}, bf16[208,768]{1,0:T(8,128)(2,1)S(1)}, bf16[208,1152]{1,0:T(8,128)(2,1)S(1)}, f32[3,8,208]{2,1,0:T(8,128)S(1)},...) custom-call(f32[208,768]{1,0:T(8,128)S(1)} %get-tuple-element.90.refs_0_.refs_4_, ...), custom_call_target="tpu_custom_call" | custom-call | flops 623640576 | bytes 9437184 | tf_op jit(solution)/shard_map/attention_1/pallas_call | solution.py:339
  122.8 8.8 %feed_1.1 = (bf16[768,7680]{1,0:T(8,128)(2,1)}, f32[208,768]{1,0:T(8,128)S(1)}, bf16[208,768]{1,0:T(8,128)(2,1)}, bf16[208,768]{1,0:T(8,128)(2,1)S(1)}, f32[1,1536]{1,0:T(1,128)S(1)}, /*index=5*/f32[8,768]{1,0:T(8,128)S(1)}) custom-call(bf16[208,768]{1,0:T(8,128)(2,1)S(1)} %pad.19.branch.refs_0_, f32[208,768]{1,0:T(8,128)S(1)} %get-tuple-element.92.stream, ...), custom_call_target="tpu_custom_call" | custom-call | flops 2944401408 | bytes 18874368 | tf_op jit(solution)/shard_map/feed_1/pallas_call | solution.py:339
  133.2 9.1 %attention_back_1.1 = (bf16[768,7680]{1,0:T(8,128)(2,1)}, f32[208,768]{1,0:T(8,128)S(1)}, bf16[208,768]{1,0:T(8,128)(2,1)S(1)}, f32[8,768]{1,0:T(8,128)S(1)}, f32[1,1152]{1,0:T(1,128)S(1)}) custom-call(bf16[208,768]{1,0:T(8,128)(2,1)S(1)} %pad.19.branch.refs_0_, bf16[208,768]{1,0:T(8,128)(2,1)S(1)} %get-tuple-element.94.refs_1_, ...), custom_call_target="tpu_custom_call", output_to_operand_aliasing={{0}: (10, {})} | custom-call | flops 1313734656 | bytes 9437184 | tf_op jit(solution)/shard_map/attention_back_1/pallas_call | solution.py:339
  143.9 8.0 %feed_back_0.1 = (bf16[768,7680]{1,0:T(8,128)(2,1)}, bf16[208,768]{1,0:T(8,128)(2,1)S(1)}, f32[1,1536]{1,0:T(1,128)S(1)}, f32[8,768]{1,0:T(8,128)S(1)}, bf16[208,768]{1,0:T(8,128)(2,1)S(1)}) custom-call(f32[208,768]{1,0:T(8,128)S(1)} %get-tuple-element.101.grad, bf16[208,768]{1,0:T(8,128)(2,1)S(1)} %get-tuple-element.102.own, ...), custom_call_target="tpu_custom_call", output_to_operand_aliasing={{0}: (8, {})} | custom-call | flops 1962934272 | bytes 18874368 | tf_op jit(solution)/shard_map/feed_back_0/pallas_call | solution.py:339
  158.9 9.3 %attention_back_0.1 = (bf16[2,4,48,768]{3,2,1,0:T(8,128)(2,1)S(1)}, bf16[2,4,48,768]{3,2,1,0:T(8,128)(2,1)}, bf16[2,4,48,768]{3,2,1,0:T(8,128)(2,1)S(1)}, bf16[2...) custom-call(s32[8]{0:T(128)S(1)} %pad_add_fusion.refs_0_, ...), custom_call_target="tpu_custom_call" | custom-call | flops 1313734656 | bytes 9437184 | tf_op jit(solution)/shard_map/attention_back_0/pallas_call | solution.py:339
  171.7 2.7 last.1
  174.4 2.5 collective-permute-start.29
  176.9 5.7 %collective-permute-done.29 = f32[32,768]{1,0:T(8,128)S(1)} collective-permute-done((f32[32,768]{1,0:T(8,128)S(1)}, f32[32,768]{1,0:T(8,128)S(1)}, u32[]{:S(2)}, u32[]{:S(2)}) %collective-permute-start.29) | collective-permute-done | bytes 98336 | tf_op jit(solution)/shard_map/ppermute | solution.py:467
  183.9 2.6 collective-permute-start.27
  186.4 11.3 %collective-permute-done.30 = f32[32,768]{1,0:T(8,128)S(1)} collective-permute-done((f32[32,768]{1,0:T(8,128)S(1)}, f32[32,768]{1,0:T(8,128)S(1)}, u32[]{:S(2)}, u32[]{:S(2)}) %collective-permute-start.30) | collective-permute-done | bytes 98336 | tf_op jit(solution)/shard_map/ppermute | solution.py:467
  201.8 2.7 collective-permute-done.31
  206.9 4.7 %collective-permute-done.32 = f32[32,768]{1,0:T(8,128)S(1)} collective-permute-done((f32[32,768]{1,0:T(8,128)S(1)}, f32[32,768]{1,0:T(8,128)S(1)}, u32[]{:S(2)}, u32[]{:S(2)}) %collective-permute-start.32) | collective-permute-done | bytes 98336 | tf_op jit(solution)/shard_map/ppermute | solution.py:467
  211.6 2.5 collective-permute-start.33
  214.5 2.3 collective-permute-done.33
  218.0 8.2 %collective-permute-done.34 = f32[32,768]{1,0:T(8,128)S(1)} collective-permute-done((f32[32,768]{1,0:T(8,128)S(1)}, f32[32,768]{1,0:T(8,128)S(1)}, u32[]{:S(2)}, u32[]{:S(2)}) %collective-permute-start.34) | collective-permute-done | bytes 98336 | tf_op jit(solution)/shard_map/ppermute | solution.py:467
  226.3 4.7 %collective-permute-start.35 = (f32[3,768]{1,0:T(4,128)S(1)}, f32[3,768]{1,0:T(4,128)S(1)}, u32[]{:S(2)}, u32[]{:S(2)}) collective-permute-start(f32[3,768]{1,0:T(4,128)S(1)} %slice_select_fusion.2), channel_id=1, source_target_pairs={{0,64},{64,0},{1,65},{65,1},{2,66},{66,2},{3,67},{67,3},{4,68},{68... | collective-permute-start | bytes 27656 | tf_op jit(solution)/shard_map/ppermute | solution.py:454
  239.8 3.9 %collective-permute-done.23 = bf16[48,1536]{1,0:T(8,128)(2,1)S(1)} collective-permute-done((bf16[48,1536]{1,0:T(8,128)(2,1)S(1)}, bf16[48,1536]{1,0:T(8,128)(2,1)S(1)}, u32[]{:S(2)}, u32[]{:S(2)}) %collective-permute-start.23) | collective-permute-done | bytes 147488 | tf_op jit(solution)/shard_map/ppermute | solution.py:467
  248.3 8.3 %reduce-scatter.2.cloned.1.call-done = bf16[48,7680]{1,0:T(8,128)(2,1)} async-done(((bf16[768,7680]{1,0:T(8,128)(2,1)}), bf16[48,7680]{1,0:T(8,128)(2,1)}) %reduce-scatter.2.cloned.1.call-update) | async-done | bytes 737296 | tf_op jit(solution)/shard_map/reduce_scatter | solution.py:577
  256.6 2.7 collective-permute-start.36
  259.3 9.1 %collective-permute-done.36 = bf16[48,7680]{1,0:T(8,128)(2,1)S(1)} collective-permute-done((bf16[48,7680]{1,0:T(8,128)(2,1)}, bf16[48,7680]{1,0:T(8,128)(2,1)S(1)}, u32[]{:S(2)}, u32[]{:S(2)}) %collective-permute-start.36) | collective-permute-done | bytes 737312 | tf_op jit(solution)/shard_map/ppermute | solution.py:467
  271.3 9.1 %collective-permute-done.37 = bf16[48,7680]{1,0:T(8,128)(2,1)S(1)} collective-permute-done((bf16[48,7680]{1,0:T(8,128)(2,1)S(1)}, bf16[48,7680]{1,0:T(8,128)(2,1)S(1)}, u32[]{:S(2)}, u32[]{:S(2)}) %collective-permute-start.37) | collective-permute-done | bytes 737312 | tf_op jit(solution)/shard_map/ppermute | solution.py:467
  280.7 3.0 %collective-permute-start.38 = (bf16[48,4608]{1,0:T(8,128)(2,1)S(1)}, bf16[48,4608]{1,0:T(8,128)(2,1)S(1)}, u32[]{:S(2)}, u32[]{:S(2)}) collective-permute-start(bf16[48,4608]{1,0:T(8,128)(2,1)S(1)} %broadcast_select_fusion.2), channel_id=1, source_target_pairs={{0,64},{64,0},{1,65},{65,1},{2,66},{66,2},{3,67},{67,3},{4,68},{68... | collective-permute-start | bytes 1327112 | tf_op jit(solution)/shard_map/ppermute | solution.py:454
  (231 shorter events, 66.8 us)
Async XLA Ops:
  7.2 101.3 %all-gather.4.cloned.1.call-start = ((), (), s32[]{:S(2)}) async-start(), calls=%async_computation.1 | async-start | bytes 12533760 | tf_op jit(solution)/shard_map/all_gather | solution.py:522
  15.7 240.9 %reduce-scatter.2.cloned.1.call-start = ((), (), s32[]{:S(2)}) async-start(), calls=%async_computation.2 | async-start | bytes 12533760 | tf_op jit(solution)/shard_map/reduce_scatter | solution.py:577
  17.1 7.4 %collective-permute-start.5 = (bf16[48,768]{1,0:T(8,128)(2,1)S(1)}, bf16[48,768]{1,0:T(8,128)(2,1)S(1)}, u32[]{:S(2)}, u32[]{:S(2)}) collective-permute-start(bf16[48,768]{1,0:T(8,128)(2,1)S(1)} %get-tuple-element.163), channel_id=1, source_target_pairs={{0,4},{1,5},{2,6},{3,7},{4,0},{5,1},{6,2},{7,3},{8,12},{9,13},{10,... | collective-permute-start | bytes 221192 | tf_op jit(solution)/shard_map/ppermute | solution.py:467
  20.0 4.6 %collective-permute-start.1 = (bf16[48,768]{1,0:T(8,128)(2,1)S(1)}, bf16[48,768]{1,0:T(8,128)(2,1)S(1)}, u32[]{:S(2)}, u32[]{:S(2)}) collective-permute-start(bf16[48,768]{1,0:T(8,128)(2,1)S(1)} %get-tuple-element.164), channel_id=1, source_target_pairs={{0,16},{1,17},{2,18},{3,19},{4,20},{5,21},{6,22},{7,23},{8,24},{9,... | collective-permute-start | bytes 221192 | tf_op jit(solution)/shard_map/ppermute | solution.py:467
  28.7 13.4 %collective-permute-start.7 = (bf16[4,48,768]{2,1,0:T(8,128)(2,1)S(1)}, bf16[4,48,768]{2,1,0:T(8,128)(2,1)S(1)}, u32[]{:S(2)}, u32[]{:S(2)}) collective-permute-start(bf16[4,48,768]{2,1,0:T(8,128)(2,1)S(1)} %get-tuple-element.166), channel_id=1, source_target_pairs={{0,16},{1,17},{2,18},{3,19},{4,20},{5,21},{6,22},{7,23},{8,24},{9,... | collective-permute-start | bytes 884744 | tf_op jit(solution)/shard_map/ppermute | solution.py:467
  29.0 13.4 %collective-permute-start.3 = (bf16[4,48,768]{2,1,0:T(8,128)(2,1)S(1)}, bf16[4,48,768]{2,1,0:T(8,128)(2,1)S(1)}, u32[]{:S(2)}, u32[]{:S(2)}) collective-permute-start(bf16[4,48,768]{2,1,0:T(8,128)(2,1)S(1)} %get-tuple-element.168), channel_id=1, source_target_pairs={{0,4},{1,5},{2,6},{3,7},{4,0},{5,1},{6,2},{7,3},{8,12},{9,13},{10,... | collective-permute-start | bytes 884744 | tf_op jit(solution)/shard_map/ppermute | solution.py:467
  42.1 10.6 %collective-permute-start.8 = (bf16[2,4,48,768]{3,2,1,0:T(8,128)(2,1)S(1)}, bf16[2,4,48,768]{3,2,1,0:T(8,128)(2,1)}, u32[]{:S(2)}, u32[]{:S(2)}) collective-permute-start(bf16[2,4,48,768]{3,2,1,0:T(8,128)(2,1)S(1)} %pad_maximum_fusion.3.refs_6_), channel_id=1, source_target_pairs={{0,48},{1,49},{2,50},{3,51},{4,52},{5,53},{6,54},{7,55},{8,56},{9,... | collective-permute-start | bytes 1769480 | tf_op jit(solution)/shard_map/ppermute | solution.py:467
  42.4 11.7 %collective-permute-start.4 = (bf16[2,4,48,768]{3,2,1,0:T(8,128)(2,1)S(1)}, bf16[2,4,48,768]{3,2,1,0:T(8,128)(2,1)}, u32[]{:S(2)}, u32[]{:S(2)}) collective-permute-start(bf16[2,4,48,768]{3,2,1,0:T(8,128)(2,1)S(1)} %pad_maximum_fusion.2.refs_4_), channel_id=1, source_target_pairs={{0,12},{1,13},{2,14},{3,15},{4,8},{5,9},{6,10},{7,11},{8,4},{9,5},... | collective-permute-start | bytes 1769480 | tf_op jit(solution)/shard_map/ppermute | solution.py:467
  61.5 5.8 %collective-permute-start.9 = (bf16[208,768]{1,0:T(8,128)(2,1)S(1)}, bf16[208,768]{1,0:T(8,128)(2,1)S(1)}, u32[]{:S(2)}, u32[]{:S(2)}) collective-permute-start(bf16[208,768]{1,0:T(8,128)(2,1)S(1)} %get-tuple-element.89.own), channel_id=1, source_target_pairs={{0,64},{64,0},{1,65},{65,1},{2,66},{66,2},{3,67},{67,3},{4,68},{68... | collective-permute-start | bytes 958472 | tf_op jit(solution)/shard_map/ppermute | solution.py:454
  154.8 16.8 %collective-permute-start.26 = (bf16[208,768]{1,0:T(8,128)(2,1)}, bf16[208,768]{1,0:T(8,128)(2,1)}, u32[]{:S(2)}, u32[]{:S(2)}) collective-permute-start(bf16[208,768]{1,0:T(8,128)(2,1)} %get-tuple-element.121.mixed), channel_id=1, source_target_pairs={{0,64},{64,0},{1,65},{65,1},{2,66},{66,2},{3,67},{67,3},{4,68},{68... | collective-permute-start | bytes 958472 | tf_op jit(solution)/shard_map/ppermute | solution.py:454
  170.2 29.0 %collective-permute-start.19 = (bf16[2,4,48,768]{3,2,1,0:T(8,128)(2,1)}, bf16[2,4,48,768]{3,2,1,0:T(8,128)(2,1)}, u32[]{:S(2)}, u32[]{:S(2)}) collective-permute-start(bf16[2,4,48,768]{3,2,1,0:T(8,128)(2,1)} %get-tuple-element.117), channel_id=1, source_target_pairs={{0,12},{1,13},{2,14},{3,15},{4,8},{5,9},{6,10},{7,11},{8,4},{9,5},... | collective-permute-start | bytes 1769480 | tf_op jit(solution)/shard_map/ppermute | solution.py:467
  171.4 33.1 %collective-permute-start.15 = (bf16[2,4,48,768]{3,2,1,0:T(8,128)(2,1)}, bf16[2,4,48,768]{3,2,1,0:T(8,128)(2,1)}, u32[]{:S(2)}, u32[]{:S(2)}) collective-permute-start(bf16[2,4,48,768]{3,2,1,0:T(8,128)(2,1)} %get-tuple-element.115), channel_id=1, source_target_pairs={{0,48},{1,49},{2,50},{3,51},{4,52},{5,53},{6,54},{7,55},{8,56},{9,... | collective-permute-start | bytes 1769480 | tf_op jit(solution)/shard_map/ppermute | solution.py:467
  174.4 8.2 %collective-permute-start.29 = (f32[32,768]{1,0:T(8,128)S(1)}, f32[32,768]{1,0:T(8,128)S(1)}, u32[]{:S(2)}, u32[]{:S(2)}) collective-permute-start(f32[32,768]{1,0:T(8,128)S(1)} %get-tuple-element.131), channel_id=1, source_target_pairs={{0,16},{1,17},{2,18},{3,19},{4,20},{5,21},{6,22},{7,23},{8,24},{9,... | collective-permute-start | bytes 294920 | tf_op jit(solution)/shard_map/ppermute | solution.py:467
  182.6 15.1 %collective-permute-start.30 = (f32[32,768]{1,0:T(8,128)S(1)}, f32[32,768]{1,0:T(8,128)S(1)}, u32[]{:S(2)}, u32[]{:S(2)}) collective-permute-start(f32[32,768]{1,0:T(8,128)S(1)} %add.132), channel_id=1, source_target_pairs={{0,48},{1,49},{2,50},{3,51},{4,52},{5,53},{6,54},{7,55},{8,56},{9,... | collective-permute-start | bytes 294920 | tf_op jit(solution)/shard_map/ppermute | solution.py:467
  183.9 30.3 %collective-permute-start.27 = (bf16[208,768]{1,0:T(8,128)(2,1)S(1)}, bf16[208,768]{1,0:T(8,128)(2,1)S(1)}, u32[]{:S(2)}, u32[]{:S(2)}) collective-permute-start(bf16[208,768]{1,0:T(8,128)(2,1)S(1)} %get-tuple-element.130), channel_id=1, source_target_pairs={{0,1},{1,0},{2,3},{3,2},{4,5},{5,4},{6,7},{7,6},{8,9},{9,8},{10,11... | collective-permute-start | bytes 958472 | tf_op jit(solution)/shard_map/ppermute | solution.py:467
  197.7 6.7 %collective-permute-start.31 = (f32[32,768]{1,0:T(8,128)S(1)}, f32[32,768]{1,0:T(8,128)S(1)}, u32[]{:S(2)}, u32[]{:S(2)}) collective-permute-start(f32[32,768]{1,0:T(8,128)S(1)} %add.133), channel_id=1, source_target_pairs={{0,4},{1,5},{2,6},{3,7},{4,0},{5,1},{6,2},{7,3},{8,12},{9,13},{10,... | collective-permute-start | bytes 294920 | tf_op jit(solution)/shard_map/ppermute | solution.py:467
  200.5 16.5 %collective-permute-start.20 = (bf16[1,4,48,768]{3,2,1,0:T(8,128)(2,1)S(1)}, bf16[1,4,48,768]{3,2,1,0:T(8,128)(2,1)S(1)}, u32[]{:S(2)}, u32[]{:S(2)}) collective-permute-start(bf16[1,4,48,768]{3,2,1,0:T(8,128)(2,1)S(1)} %get-tuple-element.150), channel_id=1, source_target_pairs={{0,4},{1,5},{2,6},{3,7},{4,0},{5,1},{6,2},{7,3},{8,12},{9,13},{10,... | collective-permute-start | bytes 884744 | tf_op jit(solution)/shard_map/ppermute | solution.py:467
  204.5 7.2 %collective-permute-start.32 = (f32[32,768]{1,0:T(8,128)S(1)}, f32[32,768]{1,0:T(8,128)S(1)}, u32[]{:S(2)}, u32[]{:S(2)}) collective-permute-start(f32[32,768]{1,0:T(8,128)S(1)} %add.134), channel_id=1, source_target_pairs={{0,12},{1,13},{2,14},{3,15},{4,8},{5,9},{6,10},{7,11},{8,4},{9,5},... | collective-permute-start | bytes 294920 | tf_op jit(solution)/shard_map/ppermute | solution.py:467
  205.8 11.6 %collective-permute-start.16 = (bf16[1,4,48,768]{3,2,1,0:T(8,128)(2,1)S(1)}, bf16[1,4,48,768]{3,2,1,0:T(8,128)(2,1)S(1)}, u32[]{:S(2)}, u32[]{:S(2)}) collective-permute-start(bf16[1,4,48,768]{3,2,1,0:T(8,128)(2,1)S(1)} %get-tuple-element.152), channel_id=1, source_target_pairs={{0,16},{1,17},{2,18},{3,19},{4,20},{5,21},{6,22},{7,23},{8,24},{9,... | collective-permute-start | bytes 884744 | tf_op jit(solution)/shard_map/ppermute | solution.py:467
  211.6 5.2 %collective-permute-start.33 = (f32[32,768]{1,0:T(8,128)S(1)}, f32[32,768]{1,0:T(8,128)S(1)}, u32[]{:S(2)}, u32[]{:S(2)}) collective-permute-start(f32[32,768]{1,0:T(8,128)S(1)} %add.135), channel_id=1, source_target_pairs={{0,1},{1,0},{2,3},{3,2},{4,5},{5,4},{6,7},{7,6},{8,9},{9,8},{10,11... | collective-permute-start | bytes 294920 | tf_op jit(solution)/shard_map/ppermute | solution.py:467
  214.2 30.3 %collective-permute-start.28 = (bf16[2,208,768]{2,1,0:T(8,128)(2,1)S(1)}, bf16[2,208,768]{2,1,0:T(8,128)(2,1)S(1)}, u32[]{:S(2)}, u32[]{:S(2)}) collective-permute-start(bf16[2,208,768]{2,1,0:T(8,128)(2,1)S(1)} %pad_maximum_fusion.1), channel_id=1, source_target_pairs={{0,3},{1,2},{2,1},{3,0},{4,7},{5,6},{6,5},{7,4},{8,11},{9,10},{10,... | collective-permute-start | bytes 1916936 | tf_op jit(solution)/shard_map/ppermute | solution.py:467
  216.8 9.4 %collective-permute-start.34 = (f32[32,768]{1,0:T(8,128)S(1)}, f32[32,768]{1,0:T(8,128)S(1)}, u32[]{:S(2)}, u32[]{:S(2)}) collective-permute-start(f32[32,768]{1,0:T(8,128)S(1)} %add.136), channel_id=1, source_target_pairs={{0,3},{1,2},{2,1},{3,0},{4,7},{5,6},{6,5},{7,4},{8,11},{9,10},{10,... | collective-permute-start | bytes 294920 | tf_op jit(solution)/shard_map/ppermute | solution.py:467
  217.0 16.4 %collective-permute-start.21 = (bf16[2,48,768]{2,1,0:T(8,128)(2,1)S(1)}, bf16[2,48,768]{2,1,0:T(8,128)(2,1)S(1)}, u32[]{:S(2)}, u32[]{:S(2)}) collective-permute-start(bf16[2,48,768]{2,1,0:T(8,128)(2,1)S(1)} %get-tuple-element.158), channel_id=1, source_target_pairs={{0,48},{1,49},{2,50},{3,51},{4,52},{5,53},{6,54},{7,55},{8,56},{9,... | collective-permute-start | bytes 442376 | tf_op jit(solution)/shard_map/ppermute | solution.py:467
  217.4 15.0 %collective-permute-start.17 = (bf16[2,48,768]{2,1,0:T(8,128)(2,1)S(1)}, bf16[2,48,768]{2,1,0:T(8,128)(2,1)S(1)}, u32[]{:S(2)}, u32[]{:S(2)}) collective-permute-start(bf16[2,48,768]{2,1,0:T(8,128)(2,1)S(1)} %get-tuple-element.160), channel_id=1, source_target_pairs={{0,12},{1,13},{2,14},{3,15},{4,8},{5,9},{6,10},{7,11},{8,4},{9,5},... | collective-permute-start | bytes 442376 | tf_op jit(solution)/shard_map/ppermute | solution.py:467
  226.3 5.5 %collective-permute-start.35 = (f32[3,768]{1,0:T(4,128)S(1)}, f32[3,768]{1,0:T(4,128)S(1)}, u32[]{:S(2)}, u32[]{:S(2)}) collective-permute-start(f32[3,768]{1,0:T(4,128)S(1)} %slice_select_fusion.2), channel_id=1, source_target_pairs={{0,64},{64,0},{1,65},{65,1},{2,66},{66,2},{3,67},{67,3},{4,68},{68... | collective-permute-start | bytes 27656 | tf_op jit(solution)/shard_map/ppermute | solution.py:454
  232.5 4.5 %collective-permute-start.18 = (bf16[1,48,768]{2,1,0:T(8,128)(2,1)S(1)}, bf16[1,48,768]{2,1,0:T(8,128)(2,1)S(1)}, u32[]{:S(2)}, u32[]{:S(2)}) collective-permute-start(bf16[1,48,768]{2,1,0:T(8,128)(2,1)S(1)} %fusion.4), channel_id=1, source_target_pairs={{0,4},{1,5},{2,6},{3,7},{4,0},{5,1},{6,2},{7,3},{8,12},{9,13},{10,... | collective-permute-start | bytes 221192 | tf_op jit(solution)/shard_map/ppermute | solution.py:467
  233.4 4.5 %collective-permute-start.22 = (bf16[1,48,768]{2,1,0:T(8,128)(2,1)S(1)}, bf16[1,48,768]{2,1,0:T(8,128)(2,1)S(1)}, u32[]{:S(2)}, u32[]{:S(2)}) collective-permute-start(bf16[1,48,768]{2,1,0:T(8,128)(2,1)S(1)} %fusion.2), channel_id=1, source_target_pairs={{0,16},{1,17},{2,18},{3,19},{4,20},{5,21},{6,22},{7,23},{8,24},{9,... | collective-permute-start | bytes 221192 | tf_op jit(solution)/shard_map/ppermute | solution.py:467
  238.0 5.7 %collective-permute-start.23 = (bf16[48,1536]{1,0:T(8,128)(2,1)S(1)}, bf16[48,1536]{1,0:T(8,128)(2,1)S(1)}, u32[]{:S(2)}, u32[]{:S(2)}) collective-permute-start(bf16[48,1536]{1,0:T(8,128)(2,1)S(1)} %constant_dynamic-update-slice_fusion.6), channel_id=1, source_target_pairs={{0,1},{1,0},{2,3},{3,2},{4,5},{5,4},{6,7},{7,6},{8,9},{9,8},{10,11... | collective-permute-start | bytes 442376 | tf_op jit(solution)/shard_map/ppermute | solution.py:467
  243.8 4.5 %collective-permute-start.24 = (bf16[48,1536]{1,0:T(8,128)(2,1)S(1)}, bf16[48,1536]{1,0:T(8,128)(2,1)S(1)}, u32[]{:S(2)}, u32[]{:S(2)}) collective-permute-start(bf16[48,1536]{1,0:T(8,128)(2,1)S(1)} %add_convert_fusion.7), channel_id=1, source_target_pairs={{0,3},{1,2},{2,1},{3,0},{4,7},{5,6},{6,5},{7,4},{8,11},{9,10},{10,... | collective-permute-start | bytes 442376 | tf_op jit(solution)/shard_map/ppermute | solution.py:467
  256.6 11.7 %collective-permute-start.36 = (bf16[48,7680]{1,0:T(8,128)(2,1)}, bf16[48,7680]{1,0:T(8,128)(2,1)S(1)}, u32[]{:S(2)}, u32[]{:S(2)}) collective-permute-start(bf16[48,7680]{1,0:T(8,128)(2,1)} %reduce-scatter.2.cloned.1.call-done), channel_id=1, source_target_pairs={{0,1},{1,0},{2,3},{3,2},{4,5},{5,4},{6,7},{7,6},{8,9},{9,8},{10,11... | collective-permute-start | bytes 2211848 | tf_op jit(solution)/shard_map/ppermute | solution.py:467
  269.6 10.7 %collective-permute-start.37 = (bf16[48,7680]{1,0:T(8,128)(2,1)S(1)}, bf16[48,7680]{1,0:T(8,128)(2,1)S(1)}, u32[]{:S(2)}, u32[]{:S(2)}) collective-permute-start(bf16[48,7680]{1,0:T(8,128)(2,1)S(1)} %add_convert_fusion.1), channel_id=1, source_target_pairs={{0,3},{1,2},{2,1},{3,0},{4,7},{5,6},{6,5},{7,4},{8,11},{9,10},{10,... | collective-permute-start | bytes 2211848 | tf_op jit(solution)/shard_map/ppermute | solution.py:467
  280.7 4.4 %collective-permute-start.38 = (bf16[48,4608]{1,0:T(8,128)(2,1)S(1)}, bf16[48,4608]{1,0:T(8,128)(2,1)S(1)}, u32[]{:S(2)}, u32[]{:S(2)}) collective-permute-start(bf16[48,4608]{1,0:T(8,128)(2,1)S(1)} %broadcast_select_fusion.2), channel_id=1, source_target_pairs={{0,64},{64,0},{1,65},{65,1},{2,66},{66,2},{3,67},{67,3},{4,68},{68... | collective-permute-start | bytes 1327112 | tf_op jit(solution)/shard_map/ppermute | solution.py:454
  (42 other events, 310.6 us)
Sparse Core Ops, SparseCore 0:
  15.8 92.6 all-gather.3
  153.6 102.9 reduce-scatter.1
where the time goes:
time: 294 us; the launch traced here: 293 us
  waiting for transfers between devices  142 us (48%)
  Pallas kernels  57.1 us (19%)
  starting transfers between devices  47.4 us (16%)
  local copies, waits for them, and re-layouts  20.2 us (7%)
  between operations  14.9 us (5%)
  other arithmetic  9.69 us (3%)
    ppermute x28, waiting for transfers between devices, trade(): return lax.ppermute(value, MESH, routes(axis, turn))  84.6 us
    pallas_call x11, Pallas kernels, call(): pl.pallas_call(kernel, name=name, grid=(grid,), in_specs=[spec(('in', k),...  57.1 us
    all_gather x1, waiting for transfers between devices, per_device(): weights = lax.all_gather(shard, 'dp', axis=0, tiled=True)  41.1 us
    ppermute x28, starting transfers between devices, trade(): return lax.ppermute(value, MESH, routes(axis, turn))  30.8 us
    ppermute x11, starting transfers between devices, swap(): return lax.ppermute(value, 'section', SWAP)  16.5 us
    unnamed x85, local copies, waits for them, and re-layouts  15.3 us
    reduce_scatter x1, waiting for transfers between devices, per_device(): joined = lax.psum_scatter(grads, 'dp', scatter_dimension=0, tiled=True)  8.33 us
    ppermute x11, waiting for transfers between devices, swap(): return lax.ppermute(value, 'section', SWAP)  8.21 us
  transfers between devices with their start and end apart: 41, of which 30 were waited for; matrix products, arithmetic and copies ran while one was open for 4% of the time, Pallas kernels for 7%

commit v1 on v0

v1 whole, which is shorter than its diff:
```python
import functools

import jax
import jax.numpy as jnp
from jax import lax
from jax.experimental import pallas as pl
from jax.experimental.pallas import tpu as pltpu
from jax.sharding import PartitionSpec as P

D = 768
HD = 64
FF = 3072
PATCHES = 196
ROWS = 208
GROUPS = 8
HALF = D // 2
HALF_FF = FF // 2
PAIR = 2 * HD
STEPS = 3
CHUNK = HALF_FF // STEPS
FEED = 2 * HALF_FF
ATTN = 4 * HALF
LAYER = FEED + ATTN
JOINED = LAYER + FEED
SIDE = 4
BLOCK = D // SIDE**2
MESH = ("section", "dp", "heads")
SWAP = [(0, 1), (1, 0)]
LIMIT = 48 * 2**20
SCALE = HD ** (-0.5)
epsilon = 1e-06
f32 = jnp.float32
low = jnp.bfloat16


def dot(left, right):
    return jnp.dot(left, right, preferred_element_type=f32)


def dot_t(left, right):
    return lax.dot_general(left, right, (((1,), (1,)), ((), ())), preferred_element_type=f32)


def t_dot(left, right):
    return lax.dot_general(left, right, (((0,), (0,)), ((), ())), preferred_element_type=f32)


def both(own, other):
    return own[...].astype(f32) + other[...].astype(f32)


def column_sum(value):
    return jnp.sum(value.astype(f32), axis=0, keepdims=True)


def stats(value):
    average = jnp.mean(value, axis=-1, keepdims=True)
    centred = value - average
    rate = lax.rsqrt(jnp.mean(centred * centred, axis=-1, keepdims=True) + epsilon)
    return centred * rate, rate


def norm_back(value, gain, grad):
    x, rate = stats(value)
    scaled = grad * gain
    inner = scaled - jnp.mean(scaled, axis=-1, keepdims=True)
    inner = inner - x * jnp.mean(scaled * x, axis=-1, keepdims=True)
    return rate * inner, column_sum(grad * x), column_sum(grad)


def gauss(value):
    return 0.5 + 0.5 * lax.erf(value * 0.7071067811865476), jnp.exp(value * value * -0.5) * 0.3989422804014327


def head_masks():
    left = lax.broadcasted_iota(jnp.int32, (ROWS, PAIR), 1) < HD
    nothing = jnp.zeros((ROWS, PAIR), low)
    return left, (lambda rows: jnp.where(left, rows, nothing), lambda rows: jnp.where(left, nothing, rows))


def raw_scores(key_rows, queries):
    scores = dot_t(key_rows, queries) * SCALE
    return jnp.where(lax.broadcasted_iota(jnp.int32, scores.shape, 0) < PATCHES, scores, -1e30)


def accumulate(step, total, part, low_out):
    @pl.when(step == 0)
    def _():
        total[...] = part

    @pl.when(step > 0)
    def _():
        total[...] += part

    @pl.when(step == STEPS - 1)
    def _():
        low_out[...] = total[...].astype(low)


def slot_rows(slots):
    for i in range(SIDE):
        for j in range(SIDE):
            yield i, j, pl.multiple_of(slots[i] * (SIDE * BLOCK) + slots[SIDE + j] * BLOCK, 16)


def place_rows(slots, pieces, weight, width):
    for i, j, row in slot_rows(slots):
        weight[pl.ds(row, BLOCK), :width] = pieces[j // 2][j % 2, i]
        weight[pl.ds(row, BLOCK), width:] = pieces[2 + i // 2][i % 2, j]


def send_rows(slots, grads, blocks, width):
    for i, j, row in slot_rows(slots):
        blocks[i // 2][i % 2, j] = grads[pl.ds(row, BLOCK), :width]
        blocks[2 + j // 2][j % 2, i] = grads[pl.ds(row, BLOCK), width:]


def column_copies(whole, parts, sems, start, size, outwards=False):
    copies = []
    for k in range(STEPS):
        ends = whole.at[:, pl.ds(start + k * size, size)], parts.at[k]
        copies.append(pltpu.make_async_copy(*(reversed(ends) if outwards else ends), sems.at[k]))
    return copies


def pair_forward(packed, write_lse):
    left, choose = head_masks()
    queries, keys, values = (packed[:, k * PAIR : (k + 1) * PAIR] for k in range(3))
    found = []
    for head in range(2):
        scores = raw_scores(keys, choose[head](queries))
        summit = jnp.max(scores, axis=0, keepdims=True)
        raised = jnp.exp(scores - summit)
        whole = jnp.sum(raised, axis=0, keepdims=True)
        write_lse(head, summit + jnp.log(whole))
        found.append(t_dot((raised * (1.0 / whole)).astype(low), values))
    return jnp.where(left, found[0], found[1]).astype(low)


def pair_backward(packed, lse, grad_pair, grad_packed):
    left, choose = head_masks()
    queries, keys, values = (packed[:, k * PAIR : (k + 1) * PAIR] for k in range(3))
    found = []
    for head in range(2):
        soft = jnp.exp(raw_scores(keys, choose[head](queries)) - lse[head : head + 1, :])
        grad_probs = dot_t(values, choose[head](grad_pair))
        within = jnp.sum(grad_probs * soft, axis=0, keepdims=True)
        grad_scores = (soft * (grad_probs - within)).astype(low)
        found.append((t_dot(grad_scores, keys) * SCALE, dot(grad_scores, queries) * SCALE, dot(soft.astype(low), grad_pair)))
    for k in range(3):
        grad_packed[:, k * PAIR : (k + 1) * PAIR] = jnp.where(left, found[0][k], found[1][k]).astype(low)
    return grad_packed[...]


def attention_zero_kernel(slots, base, norms, offset, *refs):
    pieces, (weight, normed_out, packed_out, lse_out, context_out, part_out, total) = refs[:SIDE], refs[SIDE:]
    step = pl.program_id(0)

    @pl.when(step == 0)
    def _():
        normed_out[...] = (stats(base[...])[0] * norms[0:1] + norms[2:3]).astype(low)

    place_rows(slots, pieces, weight, 2 * PAIR)
    packed = (dot(normed_out[...], weight[:, : 3 * PAIR]) + offset[...]).astype(low)
    packed_out[...] = packed

    def write_lse(head, row):
        lse_out[0, head : head + 1, :] = row

    context = pair_forward(packed, write_lse)
    context_out[...] = context
    accumulate(step, total, dot_t(context, weight[:, 3 * PAIR :]), part_out)


def attention_one_kernel(
    base, own, other, last_bias, norms, offset, weights,
    stream_out, normed_out, packed_out, lse_out, context_out, part_out, weight, sems,
):
    copies = column_copies(weights, weight, sems, 2 * FEED, 4 * PAIR)
    for copy in copies:
        copy.start()
    stream = (base[...] + (both(own, other) + last_bias[...])).astype(low).astype(f32)
    stream_out[...] = stream
    normed = (stats(stream)[0] * norms[0:1] + norms[2:3]).astype(low)
    normed_out[...] = normed
    total = 0.0
    for k in range(STEPS):
        copies[k].wait()
        at = slice(k * 3 * PAIR, (k + 1) * 3 * PAIR)
        packed = (dot(normed, weight[k, :, : 3 * PAIR]) + offset[:, at]).astype(low)
        packed_out[:, at] = packed

        def write_lse(head, row):
            lse_out[k, head : head + 1, :] = row

        context = pair_forward(packed, write_lse)
        context_out[:, k * PAIR : (k + 1) * PAIR] = context
        total = total + dot_t(context, weight[k, :, 3 * PAIR :])
    part_out[...] = total.astype(low)


def forward_kernel(
    stream, own, other, norms, bias, weights, middle_out, normed_out, upper_out, part_out, weight, kept, sems, out_sems
):
    copies = column_copies(weights, weight, sems, FEED, 2 * CHUNK)
    for copy in copies:
        copy.start()
    leaving = column_copies(upper_out, kept, out_sems, 0, CHUNK, True)
    middle = stream[...] + (both(own, other) + norms[3:4])
    middle_out[...] = middle
    normed = (stats(middle)[0] * norms[1:2] + norms[4:5]).astype(low)
    normed_out[...] = normed
    total = 0.0
    for k in range(STEPS):
        copies[k].wait()
        upper = dot(normed, weight[k, :, :CHUNK]) + bias[:, k * CHUNK : (k + 1) * CHUNK]
        kept[k] = upper
        leaving[k].start()
        hidden = (upper * gauss(upper)[0]).astype(low)
        total = total + dot_t(hidden, weight[k, :, CHUNK:])
    part_out[...] = total.astype(low)
    for copy in leaving:
        copy.wait()


def turn_kernel(
    branch, stream, own, other, norms, bias, weights,
    grads_out, middle_out, mixed_out, part_out, bias_out, rows_out, weight, grads, sems, out_sems,
):
    copies = column_copies(weights, weight, sems, 0, 2 * CHUNK)
    for copy in copies:
        copy.start()
    leaving = column_copies(grads_out, grads, out_sems, 0, 2 * CHUNK, True)
    middle = stream[...] + (both(own, other) + norms[3:4])
    middle_out[...] = middle
    normed = (stats(middle)[0] * norms[1:2] + norms[4:5]).astype(low)
    rows = branch[...]
    rows_out[2:3] = column_sum(rows)
    total = mixed = 0.0
    for k in range(STEPS):
        at = slice(k * CHUNK, (k + 1) * CHUNK)
        copies[k].wait()
        upper = dot(normed, weight[k, :, :CHUNK]) + bias[:, at]
        share, density = gauss(upper)
        hidden = (upper * share).astype(low)
        grad_upper = (dot(rows, weight[k, :, CHUNK:]) * (share + upper * density)).astype(low)
        total = total + dot_t(grad_upper, weight[k, :, :CHUNK])
        grads[k, :, :CHUNK] = t_dot(normed, grad_upper).astype(low)
        grads[k, :, CHUNK:] = t_dot(rows, hidden).astype(low)
        leaving[k].start()
        bias_out[:, at] = column_sum(grad_upper)
        mixed = mixed + dot_t(hidden, weight[k, :, CHUNK:])
    part_out[...] = total.astype(low)
    mixed_out[...] = mixed.astype(low)
    for copy in leaving:
        copy.wait()


def backward_kernel(
    grad, own, other, stream, gains, normed_in, uppers, weights, _,
    grads_out, part_out, bias_out, rows_out, branch, weight, upper, grads, sems, upper_sems, out_sems,
):
    copies = column_copies(weights, weight, sems, FEED, 2 * CHUNK)
    entering = column_copies(uppers, upper, upper_sems, 0, CHUNK)
    for pair in zip(copies, entering):
        for copy in pair:
            copy.start()
    leaving = column_copies(grads_out, grads, out_sems, FEED, 2 * CHUNK, True)
    into, gain, shift = norm_back(stream[...], gains[0:1], both(own, other))
    rows = (grad[...] + into).astype(low)
    branch[...] = rows
    rows_out[0:1] = gain
    rows_out[1:2] = shift
    rows_out[2:3] = column_sum(rows)
    normed = normed_in[...]
    total = 0.0
    for k in range(STEPS):
        entering[k].wait()
        copies[k].wait()
        upper_now = upper[k]
        share, density = gauss(upper_now)
        hidden = (upper_now * share).astype(low)
        grad_upper = (dot(rows, weight[k, :, CHUNK:]) * (share + upper_now * density)).astype(low)
        total = total + dot_t(grad_upper, weight[k, :, :CHUNK])
        grads[k, :, :CHUNK] = t_dot(normed, grad_upper).astype(low)
        grads[k, :, CHUNK:] = t_dot(rows, hidden).astype(low)
        leaving[k].start()
        bias_out[:, k * CHUNK : (k + 1) * CHUNK] = column_sum(grad_upper)
    part_out[...] = total.astype(low)
    for copy in leaving:
        copy.wait()


def attention_back_one_kernel(
    branch, own, other, middle, norms, normed_in, packed, lse, context, weights, _,
    grads_out, middle_out, part_out, rows_out, packed_out, weight, grads, grad_packed, sems, out_sems,
):
    copies = column_copies(weights, weight, sems, 2 * FEED, 4 * PAIR)
    for copy in copies:
        copy.start()
    leaving = column_copies(grads_out, grads, out_sems, 2 * FEED, 4 * PAIR, True)
    into, gain, shift = norm_back(middle[...], norms[1:2], both(own, other))
    grad_middle = branch[...].astype(f32) + into
    middle_out[...] = grad_middle
    attn = grad_middle.astype(low)
    rows_out[0:1] = gain
    rows_out[1:2] = shift
    rows_out[2:3] = column_sum(attn)
    normed = normed_in[...]
    total = 0.0
    for k in range(STEPS):
        at = slice(k * 3 * PAIR, (k + 1) * 3 * PAIR)
        copies[k].wait()
        grad_pair = dot(attn, weight[k, :, 3 * PAIR :]).astype(low)
        rows = pair_backward(packed[:, at], lse[k], grad_pair, grad_packed)
        total = total + dot_t(rows, weight[k, :, : 3 * PAIR])
        grads[k, :, : 3 * PAIR] = t_dot(normed, rows).astype(low)
        grads[k, :, 3 * PAIR :] = t_dot(attn, context[:, k * PAIR : (k + 1) * PAIR]).astype(low)
        leaving[k].start()
        packed_out[:, at] = column_sum(rows)
    part_out[...] = total.astype(low)
    for copy in leaving:
        copy.wait()


def attention_back_zero_kernel(
    slots, branch, own, other, middle, norms, normed, packed, lse, context, weight, *refs
):
    blocks, refs = refs[:SIDE], refs[SIDE:]
    middle_out, part_out, rows_out, packed_out, attn, total, grad_packed, grads = refs
    step = pl.program_id(0)

    @pl.when(step == 0)
    def _():
        into, gain, shift = norm_back(middle[...], norms[1:2], both(own, other))
        grad_middle = branch[...].astype(f32) + into
        middle_out[...] = grad_middle
        attn[...] = grad_middle.astype(low)
        rows_out[0:1] = gain
        rows_out[1:2] = shift
        rows_out[2:3] = column_sum(attn[...])

    grad_pair = dot(attn[...], weight[:, 3 * PAIR :]).astype(low)
    rows = pair_backward(packed[...], lse[0], grad_pair, grad_packed)
    accumulate(step, total, dot_t(rows, weight[:, : 3 * PAIR]), part_out)
    grads[:, : 3 * PAIR] = t_dot(normed[...], rows).astype(low)
    grads[:, 3 * PAIR :] = t_dot(attn[...], context[...]).astype(low)
    send_rows(slots, grads, blocks, 2 * PAIR)
    packed_out[...] = column_sum(rows)


def last_kernel(
    core, grad_middle, own, other, stream, norms, masked, tag, middle, mixed, mixed_other, last_bias,
    rows_one, sums_one, turn_rows, bias_one, rows_zero, sums_zero, back_rows, bias_zero, rows_out, vectors_low_out, vectors_out,
):
    into, gain, shift = norm_back(stream[...], norms[0:1], both(own, other))
    grad_zero = grad_middle[...] + into
    hidden = masked[...] > 0.5
    final = middle[...] + (both(mixed, mixed_other) + last_bias[...])
    first = core[0] == 0
    rows_out[...] = jnp.where(first, jnp.where(hidden, 0.0, grad_zero), final).astype(low)
    for at, gain_one, shift_one, attn_rows, feed_rows, sums, bias in (
        (0, gain, shift, rows_zero, back_rows, sums_zero, bias_zero),
        (9, back_rows[0:1], back_rows[1:2], rows_one, turn_rows, sums_one, bias_one),
    ):
        for k, row in enumerate((gain_one, attn_rows[0:1], shift_one, attn_rows[2:3], attn_rows[1:2], feed_rows[2:3])):
            vectors_out[at + k : at + k + 1] = row
        for k in range(STEPS):
            for part in range(2):
                to = part * HALF + k * PAIR
                vectors_out[at + 6 : at + 7, to : to + PAIR] = sums[:, (3 * k + 2 * part) * PAIR : (3 * k + 2 * part + 1) * PAIR]
        for k in range(2):
            vectors_out[at + 7 + k : at + 8 + k] = bias[:, k * D : (k + 1) * D]
    vectors_out[18:19] = column_sum(jnp.where(hidden, grad_zero, 0.0))
    table = column_sum(grad_zero)
    for group in range(GROUPS):
        vectors_out[19 + group : 20 + group] = jnp.where(tag[0] == group, table, 0.0)
    vectors_out[27:32] = jnp.zeros((5, D), f32)
    vectors_low_out[...] = jnp.zeros((BLOCK, 2 * HALF), low)
    vectors_low_out[0:32, 0:D] = vectors_out[...].astype(low)


def ends_kernel(order, parts, out):
    for k in range(SIDE):
        out[k * PATCHES : (k + 1) * PATCHES] = parts[order[k]].astype(f32)[:PATCHES]


def shards_kernel(core, qkv, out, up, down, mine_out, sent_out):
    def fill(half, target):
        for k in range(STEPS):
            at = slice(half * HALF_FF + k * CHUNK, half * HALF_FF + (k + 1) * CHUNK)
            target[:, 2 * k * CHUNK : (2 * k + 1) * CHUNK] = up[:, at].astype(low)
            target[:, (2 * k + 1) * CHUNK : (2 * k + 2) * CHUNK] = down[:, at].astype(low)
            at = slice(half * HALF + k * PAIR, half * HALF + (k + 1) * PAIR)
            for part, rows in enumerate((qkv[0, :, at], qkv[1, :, at], qkv[2, :, at], out[:, at])):
                to = FEED + (part // 2) * 2 * HALF + (2 * k + part % 2) * PAIR
                target[:, to : to + PAIR] = rows.astype(low)

    for index in range(2):
        @pl.when(core[0] == index)
        def _():
            fill(index, mine_out)
            fill(1 - index, sent_out)


def grads_kernel(
    core, first_half, second_half,
    qkv_out, out_out, up_out, down_out, qv_out, hidden_out, gains_out, biases_out, token_out, table_out,
):
    shared = first_half[:, LAYER:].astype(f32)
    for h, half in enumerate((first_half, second_half)):
        for k in range(STEPS):
            to = slice(h * HALF_FF + k * CHUNK, h * HALF_FF + (k + 1) * CHUNK)
            up_out[:, to] = half[:, 2 * k * CHUNK : (2 * k + 1) * CHUNK].astype(f32)
            down_out[:, to] = half[:, (2 * k + 1) * CHUNK : (2 * k + 2) * CHUNK].astype(f32)
            to = slice(h * HALF + k * PAIR, h * HALF + (k + 1) * PAIR)
            at = FEED + 4 * k * PAIR
            for c in range(3):
                qkv_out[c, :, to] = half[:, at + c * PAIR : at + (c + 1) * PAIR].astype(f32)
            out_out[:, to] = half[:, at + 3 * PAIR : at + 4 * PAIR].astype(f32)

    for index in range(2):
        @pl.when(core[0] == index)
        def _():
            at = 9 * index
            gains_out[...] = shared[at : at + 2]
            biases_out[...] = shared[at + 2 : at + 6]
            token_out[...] = shared[18:19, index * HALF : (index + 1) * HALF]
            table_out[...] = shared[19 : 19 + GROUPS, index * HALF : (index + 1) * HALF]
            for h, half in enumerate((first_half, second_half)):
                rows = half[:, LAYER:].astype(f32)
                for k in range(2):
                    qv_out[k : k + 1, h * HALF : (h + 1) * HALF] = rows[at + 6 : at + 7, k * HALF : (k + 1) * HALF]
                    hidden_out[:, h * HALF_FF + k * D : h * HALF_FF + (k + 1) * D] = rows[at + 7 + k : at + 8 + k]


def whole(array):
    return pl.BlockSpec(array.shape, lambda *_: (0,) * len(array.shape))


def shaped(shape, kind=f32):
    return jax.ShapeDtypeStruct(shape, kind)


def call(kernel, name, operands, outs, specs, micros, grid=STEPS, alias=None, scratch=(), limit=LIMIT):
    def spec(key, array):
        return specs.get(key) or whole(array)

    return pl.pallas_call(
        kernel,
        name=name,
        grid=(grid,),
        in_specs=[spec(("in", k), a) for k, a in enumerate(operands)],
        out_specs=[spec(("out", k), a) for k, a in enumerate(outs)],
        out_shape=outs,
        scratch_shapes=scratch,
        input_output_aliases=alias or {},
        cost_estimate=pl.CostEstimate(flops=0, bytes_accessed=int(micros * 3.6e6), transcendentals=0),
        compiler_params=pltpu.CompilerParams(vmem_limit_bytes=limit),
    )(*operands)


SMALL = pl.BlockSpec(memory_space=pltpu.SMEM)
LEFT = pl.BlockSpec(memory_space=pl.ANY)


def by_step(shape):
    return pl.BlockSpec(shape, lambda i: (0,) * (len(shape) - 1) + (i,))


ATTN_WEIGHT = by_step((D, 4 * PAIR))
ATTN_PIECE = by_step((2, SIDE, BLOCK, 2 * PAIR))
TRIPLE = by_step((ROWS, 3 * PAIR))
LSE = pl.BlockSpec((1, 8, ROWS), lambda i: (i, 0, 0))
STREAM = shaped((ROWS, D))
STREAM_LOW = shaped((ROWS, D), low)
TOTAL = pltpu.VMEM((ROWS, D), f32)


DMA = pltpu.SemaphoreType.DMA((STEPS,))
FEED_PARTS = pltpu.VMEM((STEPS, D, 2 * CHUNK), low)
ATTN_PARTS = pltpu.VMEM((STEPS, D, 4 * PAIR), low)
UPPER_PARTS = pltpu.VMEM((STEPS, ROWS, CHUNK), f32)
ATTN_KEPT = [STREAM_LOW, shaped((ROWS, 3 * HALF), low), shaped((STEPS, 8, ROWS)), shaped((ROWS, HALF), low), STREAM_LOW]
JOINED_GRADS = shaped((D, JOINED), low)


def attention_zero_call(slots, stream, norms, offset, pieces):
    operands = (slots, stream, norms, offset, *pieces)
    specs = {
        ("in", 0): SMALL, ("in", 3): by_step((1, 3 * PAIR)), ("out", 0): ATTN_WEIGHT, ("out", 2): TRIPLE, ("out", 3): LSE,
        ("out", 4): by_step((ROWS, PAIR)), **{("in", 4 + k): ATTN_PIECE for k in range(SIDE)},
    }
    return call(
        attention_zero_kernel, "attention_0", operands, [shaped((D, ATTN), low), *ATTN_KEPT], specs, 5, scratch=[TOTAL]
    )


def attention_one_call(base, own, other, last_bias, norms, offset, weights):
    return call(
        attention_one_kernel, "attention_1", (base, own, other, last_bias, norms, offset, weights), [STREAM, *ATTN_KEPT],
        {("in", 6): LEFT}, 4, grid=1, scratch=[ATTN_PARTS, DMA],
    )


def forward_call(stream, part, part_other, norms, bias_up, weights):
    return call(
        forward_kernel, "feed_0", (stream, part, part_other, norms, bias_up, weights),
        [STREAM, STREAM_LOW, shaped((ROWS, HALF_FF)), STREAM_LOW], {("in", 5): LEFT, ("out", 2): LEFT}, 4, grid=1,
        scratch=[FEED_PARTS, UPPER_PARTS, DMA, DMA],
    )


def turn_call(branch, stream, part, part_other, norms, bias_up, weights):
    return call(
        turn_kernel, "feed_1", (branch, stream, part, part_other, norms, bias_up, weights),
        [JOINED_GRADS, STREAM, STREAM_LOW, STREAM_LOW, shaped((1, HALF_FF)), shaped((8, D))],
        {("in", 6): LEFT, ("out", 0): LEFT}, 7, grid=1, scratch=[FEED_PARTS, FEED_PARTS, DMA, DMA],
    )


def backward_call(entry, normed, upper, weights, grads):
    return call(
        backward_kernel, "feed_back_0", (*entry, normed, upper, weights, grads),
        [JOINED_GRADS, STREAM_LOW, shaped((1, HALF_FF)), shaped((8, D)), STREAM_LOW],
        {("in", 6): LEFT, ("in", 7): LEFT, ("in", 8): LEFT, ("out", 0): LEFT}, 6, grid=1, alias={8: 0},
        scratch=[FEED_PARTS, UPPER_PARTS, FEED_PARTS, DMA, DMA, DMA],
    )


def attention_back_one_call(branch, part, part_other, middle, norms, normed, packed, lse, context, weights, grads):
    return call(
        attention_back_one_kernel, "attention_back_1",
        (branch, part, part_other, middle, norms, normed, packed, lse, context, weights, grads),
        [JOINED_GRADS, STREAM, STREAM_LOW, shaped((8, D)), shaped((1, 3 * HALF))],
        {("in", 9): LEFT, ("in", 10): LEFT, ("out", 0): LEFT}, 7, grid=1, alias={10: 0},
        scratch=[ATTN_PARTS, ATTN_PARTS, pltpu.VMEM((ROWS, 3 * PAIR), low), DMA, DMA],
    )


def attention_back_zero_call(slots, branch, part, part_other, middle, norms, normed, packed, lse, context, weight):
    specs = {
        ("in", 0): SMALL, ("in", 7): TRIPLE, ("in", 8): LSE, ("in", 9): by_step((ROWS, PAIR)), ("in", 10): ATTN_WEIGHT,
        ("out", SIDE + 3): by_step((1, 3 * PAIR)), **{("out", k): ATTN_PIECE for k in range(SIDE)},
    }
    made = call(
        attention_back_zero_kernel, "attention_back_0",
        (slots, branch, part, part_other, middle, norms, normed, packed, lse, context, weight),
        [*[shaped((2, SIDE, BLOCK, 2 * HALF), low)] * SIDE, STREAM, STREAM_LOW, shaped((8, D)), shaped((1, 3 * HALF))],
        specs, 9,
        scratch=[pltpu.VMEM((ROWS, D), low), TOTAL, pltpu.VMEM((ROWS, 3 * PAIR), low), pltpu.VMEM((D, 4 * PAIR), low)],
    )
    return made[:SIDE], made[SIDE:]


def swap(value):
    return lax.ppermute(value, "section", SWAP)


def routes(axis, turn):
    pairs = []
    for place in range(2 * SIDE**3):
        spot = [place // SIDE**3, place // SIDE**2 % SIDE, place // SIDE % SIDE, place % SIDE]
        spot[axis + 1] ^= 1 if spot[0] == turn else 3
        pairs.append((place, ((spot[0] * SIDE + spot[1]) * SIDE + spot[2]) * SIDE + spot[3]))
    return pairs


def trade(value, axis, turn):
    return lax.ppermute(value, MESH, routes(axis, turn))


def add(*values):
    return functools.reduce(jnp.add, (v.astype(f32) for v in values)).astype(low)


def both_of(own, axis, turn):
    return jnp.stack([own, trade(own, axis, turn)])


def gather_first(own, axis):
    pair = both_of(own, axis, 0)
    return jnp.concatenate([pair, trade(pair, axis, 1)])


def gather_second(own, axis):
    pair = both_of(own, axis, 0)
    return pair, trade(pair, axis, 1)


def halves_of(kept, got):
    middle = kept.shape[0] // 2
    return add(kept[:middle], got[:middle]), add(kept[middle:], got[middle:])


tied = lax.optimization_barrier


def per_device(
    patches, mask_flags, image_tags, mask_token, group_table, qkv_weight, query_value_bias, out_weight,
    up_weight, hidden_bias, down_weight, norm_gains, norm_biases, cotangent,
):
    place = lax.axis_index("heads")
    core = lax.axis_index("section")
    first = core == 0

    rows = qkv_weight.shape[1]
    mine, other = call(
        shards_kernel, "shards",
        (core.reshape(1), qkv_weight[0].transpose(1, 0, 2), out_weight[0].T, up_weight[0], down_weight[0].T),
        [shaped((rows, LAYER), low)] * 2, {("in", 0): SMALL}, 2, grid=1, limit=60 * 2**20,
    )
    other = swap(other)
    zero, one = jnp.where(first, mine, other), jnp.where(first, other, mine)

    def by_pair(wide):
        return [wide[:, s * 2 * HALF + k * 2 * PAIR : s * 2 * HALF + (k + 1) * 2 * PAIR] for k in range(STEPS) for s in (0, 1)]

    shard = jnp.concatenate([one[:, :FEED], zero[:, :FEED], *by_pair(one[:, FEED:])], axis=1)
    weights = lax.all_gather(shard, "dp", axis=0, tiled=True)
    pieces = gather_first(zero[:, FEED : FEED + 2 * HALF], 0), gather_first(zero[:, FEED + 2 * HALF :], 1)
    pieces = (*gather_second(pieces[0], 1), *gather_second(pieces[1], 0))
    later = (patches, mask_flags, image_tags, mask_token, group_table, cotangent, norm_gains, norm_biases, query_value_bias, hidden_bias)
    later, _ = tied((later, shard))
    patches, mask_flags, image_tags, mask_token, group_table, cotangent, norm_gains, norm_biases, query_value_bias, hidden_bias = later

    x, y = lax.axis_index("dp") // SIDE, lax.axis_index("dp") % SIDE
    flips = jnp.where(first, jnp.array([0, 1, 3, 2], jnp.int32), jnp.array([0, 3, 1, 2], jnp.int32))
    slots = jnp.concatenate([x ^ flips, y ^ flips])
    order = jnp.argmax((place ^ flips)[None, :] == jnp.arange(SIDE, dtype=jnp.int32)[:, None], axis=1).astype(jnp.int32)

    def half_of(vector):
        return jnp.where(first, vector[..., : vector.shape[-1] // 2], vector[..., vector.shape[-1] // 2 :])

    vectors = lax.all_gather(
        jnp.concatenate([norm_gains[0], norm_biases[0], query_value_bias[0], hidden_bias[0].reshape(4, D)]),
        "section", axis=0,
    )
    norms, offsets, bias_ups = [], [], []
    for layer in range(2):
        v = vectors[layer]
        norms.append(jnp.pad(v[:6], ((0, 2), (0, 0))))
        query, value = half_of(v[6:8]).reshape(2, STEPS, PAIR)
        offsets.append(jnp.stack([query, jnp.zeros_like(query), value], axis=1).reshape(1, 3 * HALF))
        bias_ups.append(half_of(v[8:12].reshape(1, FF)))

    def own(rows_of):
        return lax.dynamic_slice_in_dim(rows_of, place * PATCHES, PATCHES, 0)

    def padded(value):
        return jnp.pad(value, ((0, ROWS - PATCHES), (0, 0)))

    masked = lax.dynamic_slice_in_dim(mask_flags, place, 1, 0).reshape(PATCHES, 1).astype(f32)
    tag = lax.dynamic_slice_in_dim(image_tags, place, 1, 0)
    onehot = (tag[:, None] == jnp.arange(GROUPS, dtype=jnp.int32)[None, :]).astype(f32)
    image_row = jnp.sum(onehot.T * group_table, axis=0, keepdims=True)
    stream_zero = padded(jnp.where(masked > 0, mask_token[None, :], own(patches).astype(f32)) + image_row)
    seed, masked = padded(own(cotangent)), padded(masked)

    attn_zero, normed, packed, lse, context, part = attention_zero_call(slots, stream_zero, norms[0], offsets[0], pieces)
    middle, normed_two, upper, mixed = forward_call(stream_zero, part, swap(part), norms[0], bias_ups[0], weights)
    kept = (middle, norms[0], normed, packed, lse, context, attn_zero)
    stream_one, normed, packed, lse, context, part = attention_one_call(
        middle, mixed, swap(mixed), norms[0][5:6], norms[1], offsets[1], weights
    )
    grads, middle, mixed, part, bias_one, turn_rows = turn_call(
        seed, stream_one, part, swap(part), norms[1], bias_ups[1], weights
    )
    grads, grad_middle, part, rows_one, sums_one = attention_back_one_call(
        seed, part, swap(part), middle, norms[1], normed, packed, lse, context, weights, grads
    )
    grads, part, bias_zero, back_rows, branch = backward_call(
        (grad_middle, part, swap(part), stream_one, norms[1]), normed_two, upper, weights, grads
    )
    joined = lax.psum_scatter(grads, "dp", scatter_dimension=0, tiled=True)
    (zero, sent, zero_too, sent_too), (grad_middle, part, rows_zero, sums_zero) = attention_back_zero_call(
        slots, branch, part, swap(part), *kept
    )
    rows_out, vectors, _ = call(
        last_kernel, "last",
        (
            core.reshape(1), grad_middle, part, swap(part), stream_zero, norms[0], masked, tag, middle, mixed, swap(mixed),
            norms[1][5:6], rows_one, sums_one, turn_rows, bias_one, rows_zero, sums_zero, back_rows, bias_zero,
        ),
        [STREAM_LOW, shaped((BLOCK, D), low), shaped((32, D))], {("in", 0): SMALL, ("in", 7): SMALL}, 3, grid=1,
    )

    def trade_with(sent, vectors, axis, turn):
        got = trade(jnp.concatenate([sent.reshape(-1, BLOCK, D), vectors[None]]), axis, turn)
        return got[:-1].reshape(sent.shape), add(vectors, got[-1])

    (got, vectors), got_too = trade_with(sent, vectors, 0, 1), trade(sent_too, 1, 1)
    got, got_too, rows_out = tied((got, got_too, rows_out))
    ends = both_of(rows_out, 2, 0)
    (zero, sent), (zero_too, sent_too) = halves_of(zero, got), halves_of(zero_too, got_too)
    (got, vectors), got_too = trade_with(sent, vectors, 0, 0), trade(sent_too, 1, 0)
    got, got_too, ends = tied((got, got_too, ends))
    ends = jnp.concatenate([ends, trade(ends, 2, 1)])
    (zero, sent), (zero_too, sent_too) = halves_of(zero[0], got[0]), halves_of(zero_too[0], got_too[0])
    (got, vectors), got_too = trade_with(sent, vectors, 1, 1), trade(sent_too, 0, 1)
    (zero, sent), (zero_too, sent_too) = halves_of(zero, got), halves_of(zero_too, got_too)
    (got, vectors), got_too = trade_with(sent, vectors, 1, 0), trade(sent_too, 0, 0)
    attn_sum = jnp.concatenate([*by_pair(jnp.concatenate([add(zero[0], got[0]), add(zero_too[0], got_too[0])], axis=1)), vectors], axis=1)

    def z_sum(value):
        value = add(value, trade(value, 2, 0))
        return add(value, trade(value, 2, 1))

    attn_sum = z_sum(attn_sum)
    (ends_here,) = call(
        ends_kernel, "ends", (order, ends), [shaped((SIDE * PATCHES, D))], {("in", 0): SMALL}, 2, grid=1
    )
    joined, attn_sum, ends_here = tied((joined, attn_sum, ends_here))

    joined = z_sum(joined)
    zero = jnp.concatenate([joined[:, FEED : 2 * FEED], attn_sum], axis=1)
    one = jnp.concatenate([joined[:, :FEED], joined[:, 2 * FEED :], attn_sum[:, ATTN:]], axis=1)
    mine = jnp.where(first, zero, one)
    other = swap(jnp.where(first, one, zero))
    grad_qkv, grad_out, grad_up, grad_down, grad_qv, grad_hidden, grad_gains, grad_biases, grad_token, grad_table = call(
        grads_kernel, "grads", (core.reshape(1), jnp.where(first, mine, other), jnp.where(first, other, mine)),
        [
            shaped((3, rows, D)), shaped((rows, D)), shaped((rows, FF)), shaped((rows, FF)), shaped((2, D)), shaped((1, FF)),
            shaped((2, D)), shaped((4, D)), shaped((1, HALF)), shaped((GROUPS, HALF)),
        ],
        {("in", 0): SMALL}, 2, grid=1,
    )
    return (
        ends_here[None], grad_qkv.transpose(1, 0, 2)[None], grad_qv[None], grad_out.T[None], grad_up[None], grad_hidden,
        grad_down.T[None], grad_gains[None], grad_biases[None], grad_token[0], grad_table,
    )


def solution(mesh):
    in_specs = (
        P("dp", None), P("dp", None), P("dp"), P(), P(),
        P("section", "dp", None, None), P("section", None, None), P("section", None, "dp"),
        P("section", "dp", None), P("section", None), P("section", None, "dp"),
        P("section", None, None), P("section", None, None), P("dp", None),
    )
    out_specs = (
        P("section", "dp", None), P("section", "dp", None, None), P("section", None, None),
        P("section", None, "dp"), P("section", "dp", None), P("section", None), P("section", None, "dp"),
        P("section", None, None), P("section", None, None), P("section"), P(None, "section"),
    )
    return jax.shard_map(per_device, mesh=mesh, in_specs=in_specs, out_specs=out_specs, check_vma=False)
```

time: 294 us -> 287 us (0.976)
  starting transfers between devices: 47.4 us -> 40.2 us
  waiting for transfers between devices: 142 us -> 149 us
  local copies, waits for them, and re-layouts: 20.2 us -> 16.6 us
    ppermute x28 -> x22, waiting for transfers between devices: 84.6 us -> 96 us  [trade(): return lax.ppermute(value, MESH, routes(axis, turn))]
    ppermute x28 -> x22, starting transfers between devices: 30.8 us -> 25.4 us  [trade(): return lax.ppermute(value, MESH, routes(axis, turn))]
    reduce_scatter x1, waiting for transfers between devices: 8.33 us -> 4.22 us  [per_device(): joined = lax.psum_scatter(grads, 'dp', scatter_dimension=0, tiled=True)]
    unnamed x85 -> x82, local copies, waits for them, and re-layouts: 15.3 us -> 12.8 us
    ppermute x11 -> x10, waiting for transfers between devices: 8.21 us -> 10.2 us  [swap(): return lax.ppermute(value, 'section', SWAP)]
    ppermute x11 -> x10, starting transfers between devices: 16.5 us -> 14.7 us  [swap(): return lax.ppermute(value, 'section', SWAP)]
  transfers between devices with their start and end apart: 41 -> 34, of which waited for: 30 -> 26; matrix products, arithmetic and copies ran while one was open for 4% -> 3% of each run, Pallas kernels for 7% -> 7%
where the time goes in v1:
time: 287 us
  waiting for transfers between devices  149 us (52%)
  Pallas kernels  55 us (19%)
  starting transfers between devices  40.2 us (14%)
  local copies, waits for them, and re-layouts  16.6 us (6%)
  between operations  14.8 us (5%)
  other arithmetic  9.42 us (3%)
    ppermute x22, waiting for transfers between devices, trade(): return lax.ppermute(value, MESH, routes(axis, turn))  96 us
    pallas_call x11, Pallas kernels, call(): pl.pallas_call(kernel, name=name, grid=(grid,), in_specs=[spec(('in', k),...  55 us
    all_gather x1, waiting for transfers between devices, per_device(): weights = lax.all_gather(shard, 'dp', axis=0, tiled=True)  38.4 us
    ppermute x22, starting transfers between devices, trade(): return lax.ppermute(value, MESH, routes(axis, turn))  25.4 us
    ppermute x10, starting transfers between devices, swap(): return lax.ppermute(value, 'section', SWAP)  14.7 us
    unnamed x82, local copies, waits for them, and re-layouts  12.8 us
    ppermute x10, waiting for transfers between devices, swap(): return lax.ppermute(value, 'section', SWAP)  10.2 us
  transfers between devices with their start and end apart: 34, of which 26 were waited for; matrix products, arithmetic and copies ran while one was open for 3% of the time, Pallas kernels for 7%

profile of v1, /device:TPU:1, one launch (start us, length us, event | category | flops | bytes accessed | tf_op | source)
XLA Modules:
  0.0 286.7 jit_solution(14873923717230385798)
XLA Ops:
  7.2 2.5 shards.1
  17.1 2.9 %collective-permute-start.5 = (bf16[48,768]{1,0:T(8,128)(2,1)S(1)}, bf16[48,768]{1,0:T(8,128)(2,1)S(1)}, u32[]{:S(2)}, u32[]{:S(2)}) collective-permute-start(bf16[48,768]{1,0:T(8,128)(2,1)S(1)} %get-tuple-element.179), channel_id=1, source_target_pairs={{0,4},{1,5},{2,6},{3,7},{4,0},{5,1},{6,2},{7,3},{8,12},{9,13},{10,... | collective-permute-start | bytes 221192 | tf_op jit(solution)/shard_map/ppermute | solution.py:570
  20.0 2.5 collective-permute-start.1
  22.5 1.9 all-gather.1
  25.9 3.2 %collective-permute-done.6 = bf16[2,48,768]{2,1,0:T(8,128)(2,1)S(1)} collective-permute-done((bf16[2,48,768]{2,1,0:T(8,128)(2,1)S(1)}, bf16[2,48,768]{2,1,0:T(8,128)(2,1)S(1)}, u32[]{:S(2)}, u32[]{:S(2)}) %collective-permute-start.6) | collective-permute-done | bytes 147488 | tf_op jit(solution)/shard_map/ppermute | solution.py:570
  31.3 11.3 %collective-permute-done.7 = bf16[4,48,768]{2,1,0:T(8,128)(2,1)S(1)} collective-permute-done((bf16[4,48,768]{2,1,0:T(8,128)(2,1)S(1)}, bf16[4,48,768]{2,1,0:T(8,128)(2,1)S(1)}, u32[]{:S(2)}, u32[]{:S(2)}) %collective-permute-start.7) | collective-permute-done | bytes 294944 | tf_op jit(solution)/shard_map/ppermute | solution.py:570
  47.0 5.5 %collective-permute-done.8.refs_3_ = bf16[2,4,48,768]{3,2,1,0:T(8,128)(2,1)} collective-permute-done((bf16[2,4,48,768]{3,2,1,0:T(8,128)(2,1)S(1)}, bf16[2,4,48,768]{3,2,1,0:T(8,128)(2,1)}, u32[]{:S(2)}, u32[]{:S(2)}) %collective-permute-start.8) | collective-permute-done | bytes 589856 | tf_op jit(solution)/shard_map/ppermute | solution.py:570
  54.0 6.0 %attention_0.1 = (bf16[768,1536]{1,0:T(8,128)(2,1)}, bf16[208,768]{1,0:T(8,128)(2,1)S(1)}, bf16[208,1152]{1,0:T(8,128)(2,1)S(1)}, f32[3,8,208]{2,1,0:T(8,128)S(1...) custom-call(s32[8]{0:T(128)S(1)} %pad_add_fusion.slots, f32[208,768]{1,0:T(8,128)S(1)} %pad.20.base.stream, ...), custom_call_target="tpu_custom_call" | custom-call | bytes 18000000 | tf_op jit(solution)/shard_map/attention_0/pallas_call | solution.py:449
  61.4 6.9 %collective-permute-start.9 = (bf16[208,768]{1,0:T(8,128)(2,1)S(1)}, bf16[208,768]{1,0:T(8,128)(2,1)S(1)}, u32[]{:S(2)}, u32[]{:S(2)}) collective-permute-start(bf16[208,768]{1,0:T(8,128)(2,1)S(1)} %get-tuple-element.97.own), channel_id=1, source_target_pairs={{0,64},{64,0},{1,65},{65,1},{2,66},{66,2},{3,67},{67,3},{4,68},{68... | collective-permute-start | bytes 958472 | tf_op jit(solution)/shard_map/ppermute | solution.py:557
  69.6 38.4 %all-gather.4.cloned.1.call-done.weights = bf16[768,7680]{1,0:T(8,128)(2,1)} async-done(((bf16[48,7680]{1,0:T(8,128)(2,1)}), bf16[768,7680]{1,0:T(8,128)(2,1)}) %all-gather.4.cloned.1.call-update) | async-done | bytes 11796496 | tf_op jit(solution)/shard_map/all_gather | solution.py:620
  109.0 4.2 %feed_0.1 = (f32[208,768]{1,0:T(8,128)S(1)}, bf16[208,768]{1,0:T(8,128)(2,1)S(1)}, f32[208,1536]{1,0:T(8,128)S(1)}, bf16[208,768]{1,0:T(8,128)(2,1)S(1)}) custom-call(f32[208,768]{1,0:T(8,128)S(1)} %pad.20.base.stream, bf16[208,768]{1,0:T(8,128)(2,1)S(1)} %copy-done.16, bf16[208,768]{1,0:T(8,128)(2,1)S(1)} %collective-permute-done.9.other, ...), custom_call_target="tpu_custom_call" | custom-call | bytes 14400000 | tf_op jit(solution)/shard_map/feed_0/pallas_call | solution.py:449
  115.1 4.3 %attention_1.1 = (f32[208,768]{1,0:T(8,128)S(1)}, bf16[208,768]{1,0:T(8,128)(2,1)S(1)}, bf16[208,1152]{1,0:T(8,128)(2,1)S(1)}, f32[3,8,208]{2,1,0:T(8,128)S(1)},...) custom-call(f32[208,768]{1,0:T(8,128)S(1)} %get-tuple-element.98.base.middle, ...), custom_call_target="tpu_custom_call" | custom-call | bytes 14400000 | tf_op jit(solution)/shard_map/attention_1/pallas_call | solution.py:449
  121.3 8.0 %feed_1.1 = (bf16[768,7680]{1,0:T(8,128)(2,1)}, f32[208,768]{1,0:T(8,128)S(1)}, bf16[208,768]{1,0:T(8,128)(2,1)}, bf16[208,768]{1,0:T(8,128)(2,1)S(1)}, f32[1,1536]{1,0:T(1,128)S(1)}, /*index=5*/f32[8,768]{1,0:T(8,128)S(1)}) custom-call(bf16[208,768]{1,0:T(8,128)(2,1)S(1)} %pad.19.branch, f32[208,768]{1,0:T(8,128)S(1)} %get-tuple-element.100.stream, ...), custom_call_target="tpu_custom_call" | custom-call | bytes 25200000 | tf_op jit(solution)/shard_map/feed_1/pallas_call | solution.py:449
  131.1 7.4 %attention_back_1.1 = (bf16[768,7680]{1,0:T(8,128)(2,1)}, f32[208,768]{1,0:T(8,128)S(1)}, bf16[208,768]{1,0:T(8,128)(2,1)S(1)}, f32[8,768]{1,0:T(8,128)S(1)}, f32[1,1152]{1,0:T(1,128)S(1)}) custom-call(bf16[208,768]{1,0:T(8,128)(2,1)S(1)} %pad.19.branch, bf16[208,768]{1,0:T(8,128)(2,1)S(1)} %get-tuple-element.102.own, ...), custom_call_target="tpu_custom_call", output_to_operand_aliasing={{0}: (10, {})} | custom-call | bytes 25200000 | tf_op jit(solution)/shard_map/attention_back_1/pallas_call | solution.py:449
  140.4 6.4 %feed_back_0.1 = (bf16[768,7680]{1,0:T(8,128)(2,1)}, bf16[208,768]{1,0:T(8,128)(2,1)S(1)}, f32[1,1536]{1,0:T(1,128)S(1)}, f32[8,768]{1,0:T(8,128)S(1)}, bf16[208,768]{1,0:T(8,128)(2,1)S(1)}) custom-call(f32[208,768]{1,0:T(8,128)S(1)} %get-tuple-element.109.grad, bf16[208,768]{1,0:T(8,128)(2,1)S(1)} %get-tuple-element.110.own, ...), custom_call_target="tpu_custom_call", output_to_operand_aliasing={{0}: (8, {})} | custom-call | bytes 21600000 | tf_op jit(solution)/shard_map/feed_back_0/pallas_call | solution.py:449
  153.7 9.3 %attention_back_0.1 = (bf16[2,4,48,768]{3,2,1,0:T(8,128)(2,1)S(1)}, bf16[2,4,48,768]{3,2,1,0:T(8,128)(2,1)S(1)}, bf16[2,4,48,768]{3,2,1,0:T(8,128)(2,1)S(1)}, bf...) custom-call(s32[8]{0:T(128)S(1)} %pad_add_fusion.slots, ...), custom_call_target="tpu_custom_call" | custom-call | bytes 32400000 | tf_op jit(solution)/shard_map/attention_back_0/pallas_call | solution.py:449
  168.1 3.4 %last.1 = (bf16[208,768]{1,0:T(8,128)(2,1)S(1)}, bf16[48,768]{1,0:T(8,128)(2,1)S(1)}, f32[32,768]{1,0:T(8,128)}) custom-call(s32[1]{0:T(128)} %bitcast.core, f32[208,768]{1,0:T(8,128)S(1)} %get-tuple-element.124.grad_middle, bf16[208,768]{1,0:T(8,128)(2,1)} %get-tuple-element.125.own, bf16[208,768]{1,0:T(8,128)(2,1)S(1)} %collective-permute-done.15.other, ...), custom_call_target="tpu_custom_call" | custom-call | bytes 10800000 | tf_op jit(solution)/shard_map/last/pallas_call | solution.py:449
  172.8 22.5 %collective-permute-done.17 = bf16[9,48,768]{2,1,0:T(8,128)(2,1)S(1)} collective-permute-done((bf16[9,48,768]{2,1,0:T(8,128)(2,1)S(1)}, bf16[9,48,768]{2,1,0:T(8,128)(2,1)S(1)}, u32[]{:S(2)}, u32[]{:S(2)}) %collective-permute-start.17) | collective-permute-done | bytes 663584 | tf_op jit(solution)/shard_map/ppermute | solution.py:570
  195.4 2.8 collective-permute-start.21
  198.4 2.8 collective-permute-start.19
  203.0 11.3 %collective-permute-done.19 = bf16[5,48,768]{2,1,0:T(8,128)(2,1)S(1)} collective-permute-done((bf16[5,48,768]{2,1,0:T(8,128)(2,1)S(1)}, bf16[5,48,768]{2,1,0:T(8,128)(2,1)S(1)}, u32[]{:S(2)}, u32[]{:S(2)}) %collective-permute-start.19) | collective-permute-done | bytes 368672 | tf_op jit(solution)/shard_map/ppermute | solution.py:570
  215.7 5.3 %collective-permute-done.24 = bf16[2,48,768]{2,1,0:T(8,128)(2,1)S(1)} collective-permute-done((bf16[2,48,768]{2,1,0:T(8,128)(2,1)S(1)}, bf16[2,48,768]{2,1,0:T(8,128)(2,1)S(1)}, u32[]{:S(2)}, u32[]{:S(2)}) %collective-permute-start.24) | collective-permute-done | bytes 147488 | tf_op jit(solution)/shard_map/ppermute | solution.py:570
  225.5 2.4 collective-permute-done.23
  228.1 2.3 collective-permute-start.26
  230.4 4.0 %collective-permute-done.26 = bf16[48,2304]{1,0:T(8,128)(2,1)S(1)} collective-permute-done((bf16[48,2304]{1,0:T(8,128)(2,1)S(1)}, bf16[48,2304]{1,0:T(8,128)(2,1)S(1)}, u32[]{:S(2)}, u32[]{:S(2)}) %collective-permute-start.26) | collective-permute-done | bytes 221216 | tf_op jit(solution)/shard_map/ppermute | solution.py:570
  235.2 7.2 %collective-permute-done.28 = bf16[2,208,768]{2,1,0:T(8,128)(2,1)S(1)} collective-permute-done((bf16[2,208,768]{2,1,0:T(8,128)(2,1)S(1)}, bf16[2,208,768]{2,1,0:T(8,128)(2,1)S(1)}, u32[]{:S(2)}, u32[]{:S(2)}) %collective-permute-start.28) | collective-permute-done | bytes 639008 | tf_op jit(solution)/shard_map/ppermute | solution.py:570
  242.5 2.2 ends.1
  244.8 4.2 %reduce-scatter.2.cloned.1.call-done = bf16[48,7680]{1,0:T(8,128)(2,1)} async-done(((bf16[768,7680]{1,0:T(8,128)(2,1)}), bf16[48,7680]{1,0:T(8,128)(2,1)}) %reduce-scatter.2.cloned.1.call-update) | async-done | bytes 737296 | tf_op jit(solution)/shard_map/reduce_scatter | solution.py:675
  249.0 2.7 collective-permute-start.29
  251.7 9.1 %collective-permute-done.29 = bf16[48,7680]{1,0:T(8,128)(2,1)S(1)} collective-permute-done((bf16[48,7680]{1,0:T(8,128)(2,1)}, bf16[48,7680]{1,0:T(8,128)(2,1)S(1)}, u32[]{:S(2)}, u32[]{:S(2)}) %collective-permute-start.29) | collective-permute-done | bytes 737312 | tf_op jit(solution)/shard_map/ppermute | solution.py:570
  262.5 10.3 %collective-permute-done.30 = bf16[48,7680]{1,0:T(8,128)(2,1)S(1)} collective-permute-done((bf16[48,7680]{1,0:T(8,128)(2,1)S(1)}, bf16[48,7680]{1,0:T(8,128)(2,1)S(1)}, u32[]{:S(2)}, u32[]{:S(2)}) %collective-permute-start.30) | collective-permute-done | bytes 737312 | tf_op jit(solution)/shard_map/ppermute | solution.py:570
  273.1 3.0 %collective-permute-start.31 = (bf16[48,5376]{1,0:T(8,128)(2,1)S(1)}, bf16[48,5376]{1,0:T(8,128)(2,1)S(1)}, u32[]{:S(2)}, u32[]{:S(2)}) collective-permute-start(bf16[48,5376]{1,0:T(8,128)(2,1)S(1)} %broadcast_select_fusion.2), channel_id=1, source_target_pairs={{0,64},{64,0},{1,65},{65,1},{2,66},{66,2},{3,67},{67,3},{4,68},{68... | collective-permute-start | bytes 1548296 | tf_op jit(solution)/shard_map/ppermute | solution.py:557
  (205 shorter events, 56.0 us)
Async XLA Ops:
  7.2 100.8 %all-gather.4.cloned.1.call-start = ((), (), s32[]{:S(2)}) async-start(), calls=%async_computation.1 | async-start | bytes 12533760 | tf_op jit(solution)/shard_map/all_gather | solution.py:620
  9.8 3.1 %collective-permute-start = (bf16[48,4608]{1,0:T(8,128)(2,1)}, bf16[48,4608]{1,0:T(8,128)(2,1)S(1)}, u32[]{:S(2)}, u32[]{:S(2)}) collective-permute-start(bf16[48,4608]{1,0:T(8,128)(2,1)} %get-tuple-element.85), channel_id=1, source_target_pairs={{0,64},{64,0},{1,65},{65,1},{2,66},{66,2},{3,67},{67,3},{4,68},{68... | collective-permute-start | bytes 1327112 | tf_op jit(solution)/shard_map/ppermute | solution.py:557
  15.1 233.9 %reduce-scatter.2.cloned.1.call-start = ((), (), s32[]{:S(2)}) async-start(), calls=%async_computation.2 | async-start | bytes 12533760 | tf_op jit(solution)/shard_map/reduce_scatter | solution.py:675
  17.1 8.0 %collective-permute-start.5 = (bf16[48,768]{1,0:T(8,128)(2,1)S(1)}, bf16[48,768]{1,0:T(8,128)(2,1)S(1)}, u32[]{:S(2)}, u32[]{:S(2)}) collective-permute-start(bf16[48,768]{1,0:T(8,128)(2,1)S(1)} %get-tuple-element.179), channel_id=1, source_target_pairs={{0,4},{1,5},{2,6},{3,7},{4,0},{5,1},{6,2},{7,3},{8,12},{9,13},{10,... | collective-permute-start | bytes 221192 | tf_op jit(solution)/shard_map/ppermute | solution.py:570
  20.0 5.2 %collective-permute-start.1 = (bf16[48,768]{1,0:T(8,128)(2,1)S(1)}, bf16[48,768]{1,0:T(8,128)(2,1)S(1)}, u32[]{:S(2)}, u32[]{:S(2)}) collective-permute-start(bf16[48,768]{1,0:T(8,128)(2,1)S(1)} %get-tuple-element.180), channel_id=1, source_target_pairs={{0,16},{1,17},{2,18},{3,19},{4,20},{5,21},{6,22},{7,23},{8,24},{9,... | collective-permute-start | bytes 221192 | tf_op jit(solution)/shard_map/ppermute | solution.py:570
  25.1 4.1 %collective-permute-start.6 = (bf16[2,48,768]{2,1,0:T(8,128)(2,1)S(1)}, bf16[2,48,768]{2,1,0:T(8,128)(2,1)S(1)}, u32[]{:S(2)}, u32[]{:S(2)}) collective-permute-start(bf16[2,48,768]{2,1,0:T(8,128)(2,1)S(1)} %pad_maximum_fusion.12), channel_id=1, source_target_pairs={{0,12},{1,13},{2,14},{3,15},{4,8},{5,9},{6,10},{7,11},{8,4},{9,5},... | collective-permute-start | bytes 442376 | tf_op jit(solution)/shard_map/ppermute | solution.py:570
  25.2 4.3 %collective-permute-start.2 = (bf16[2,48,768]{2,1,0:T(8,128)(2,1)S(1)}, bf16[2,48,768]{2,1,0:T(8,128)(2,1)S(1)}, u32[]{:S(2)}, u32[]{:S(2)}) collective-permute-start(bf16[2,48,768]{2,1,0:T(8,128)(2,1)S(1)} %pad_maximum_fusion.11), channel_id=1, source_target_pairs={{0,48},{1,49},{2,50},{3,51},{4,52},{5,53},{6,54},{7,55},{8,56},{9,... | collective-permute-start | bytes 442376 | tf_op jit(solution)/shard_map/ppermute | solution.py:570
  29.2 13.4 %collective-permute-start.7 = (bf16[4,48,768]{2,1,0:T(8,128)(2,1)S(1)}, bf16[4,48,768]{2,1,0:T(8,128)(2,1)S(1)}, u32[]{:S(2)}, u32[]{:S(2)}) collective-permute-start(bf16[4,48,768]{2,1,0:T(8,128)(2,1)S(1)} %get-tuple-element.182), channel_id=1, source_target_pairs={{0,16},{1,17},{2,18},{3,19},{4,20},{5,21},{6,22},{7,23},{8,24},{9,... | collective-permute-start | bytes 884744 | tf_op jit(solution)/shard_map/ppermute | solution.py:570
  29.5 13.2 %collective-permute-start.3 = (bf16[4,48,768]{2,1,0:T(8,128)(2,1)S(1)}, bf16[4,48,768]{2,1,0:T(8,128)(2,1)S(1)}, u32[]{:S(2)}, u32[]{:S(2)}) collective-permute-start(bf16[4,48,768]{2,1,0:T(8,128)(2,1)S(1)} %get-tuple-element.184), channel_id=1, source_target_pairs={{0,4},{1,5},{2,6},{3,7},{4,0},{5,1},{6,2},{7,3},{8,12},{9,13},{10,... | collective-permute-start | bytes 884744 | tf_op jit(solution)/shard_map/ppermute | solution.py:570
  42.7 9.8 %collective-permute-start.8 = (bf16[2,4,48,768]{3,2,1,0:T(8,128)(2,1)S(1)}, bf16[2,4,48,768]{3,2,1,0:T(8,128)(2,1)}, u32[]{:S(2)}, u32[]{:S(2)}) collective-permute-start(bf16[2,4,48,768]{3,2,1,0:T(8,128)(2,1)S(1)} %pad_maximum_fusion.4.refs_2_), channel_id=1, source_target_pairs={{0,48},{1,49},{2,50},{3,51},{4,52},{5,53},{6,54},{7,55},{8,56},{9,... | collective-permute-start | bytes 1769480 | tf_op jit(solution)/shard_map/ppermute | solution.py:570
  42.8 11.2 %collective-permute-start.4 = (bf16[2,4,48,768]{3,2,1,0:T(8,128)(2,1)S(1)}, bf16[2,4,48,768]{3,2,1,0:T(8,128)(2,1)}, u32[]{:S(2)}, u32[]{:S(2)}) collective-permute-start(bf16[2,4,48,768]{3,2,1,0:T(8,128)(2,1)S(1)} %pad_maximum_fusion.3.refs_0_), channel_id=1, source_target_pairs={{0,12},{1,13},{2,14},{3,15},{4,8},{5,9},{6,10},{7,11},{8,4},{9,5},... | collective-permute-start | bytes 1769480 | tf_op jit(solution)/shard_map/ppermute | solution.py:570
  61.4 8.2 %collective-permute-start.9 = (bf16[208,768]{1,0:T(8,128)(2,1)S(1)}, bf16[208,768]{1,0:T(8,128)(2,1)S(1)}, u32[]{:S(2)}, u32[]{:S(2)}) collective-permute-start(bf16[208,768]{1,0:T(8,128)(2,1)S(1)} %get-tuple-element.97.own), channel_id=1, source_target_pairs={{0,64},{64,0},{1,65},{65,1},{2,66},{66,2},{3,67},{67,3},{4,68},{68... | collective-permute-start | bytes 958472 | tf_op jit(solution)/shard_map/ppermute | solution.py:557
  113.1 2.0 collective-permute-start.10
  119.5 1.9 collective-permute-start.11
  138.5 1.9 collective-permute-start.13
  149.6 17.2 %collective-permute-start.16 = (bf16[208,768]{1,0:T(8,128)(2,1)}, bf16[208,768]{1,0:T(8,128)(2,1)}, u32[]{:S(2)}, u32[]{:S(2)}) collective-permute-start(bf16[208,768]{1,0:T(8,128)(2,1)} %get-tuple-element.126.mixed), channel_id=1, source_target_pairs={{0,64},{64,0},{1,65},{65,1},{2,66},{66,2},{3,67},{67,3},{4,68},{68... | collective-permute-start | bytes 958472 | tf_op jit(solution)/shard_map/ppermute | solution.py:557
  166.2 1.8 collective-permute-start.15
  171.5 23.8 %collective-permute-start.17 = (bf16[9,48,768]{2,1,0:T(8,128)(2,1)S(1)}, bf16[9,48,768]{2,1,0:T(8,128)(2,1)S(1)}, u32[]{:S(2)}, u32[]{:S(2)}) collective-permute-start(bf16[9,48,768]{2,1,0:T(8,128)(2,1)S(1)} %pad_maximum_fusion.1), channel_id=1, source_target_pairs={{0,48},{1,49},{2,50},{3,51},{4,52},{5,53},{6,54},{7,55},{8,56},{9,... | collective-permute-start | bytes 1990664 | tf_op jit(solution)/shard_map/ppermute | solution.py:570
  172.7 22.7 %collective-permute-start.18 = (bf16[2,4,48,768]{3,2,1,0:T(8,128)(2,1)S(1)}, bf16[2,4,48,768]{3,2,1,0:T(8,128)(2,1)S(1)}, u32[]{:S(2)}, u32[]{:S(2)}) collective-permute-start(bf16[2,4,48,768]{3,2,1,0:T(8,128)(2,1)S(1)} %copy-done.20), channel_id=1, source_target_pairs={{0,12},{1,13},{2,14},{3,15},{4,8},{5,9},{6,10},{7,11},{8,4},{9,5},... | collective-permute-start | bytes 1769480 | tf_op jit(solution)/shard_map/ppermute | solution.py:570
  195.4 7.5 %collective-permute-start.21 = (bf16[208,768]{1,0:T(8,128)(2,1)S(1)}, bf16[208,768]{1,0:T(8,128)(2,1)S(1)}, u32[]{:S(2)}, u32[]{:S(2)}) collective-permute-start(bf16[208,768]{1,0:T(8,128)(2,1)S(1)} %get-tuple-element.141), channel_id=1, source_target_pairs={{0,1},{1,0},{2,3},{3,2},{4,5},{5,4},{6,7},{7,6},{8,9},{9,8},{10,11... | collective-permute-start | bytes 958472 | tf_op jit(solution)/shard_map/ppermute | solution.py:570
  198.4 15.9 %collective-permute-start.19 = (bf16[5,48,768]{2,1,0:T(8,128)(2,1)S(1)}, bf16[5,48,768]{2,1,0:T(8,128)(2,1)S(1)}, u32[]{:S(2)}, u32[]{:S(2)}) collective-permute-start(bf16[5,48,768]{2,1,0:T(8,128)(2,1)S(1)} %pad_maximum_fusion.7), channel_id=1, source_target_pairs={{0,16},{1,17},{2,18},{3,19},{4,20},{5,21},{6,22},{7,23},{8,24},{9,... | collective-permute-start | bytes 1105928 | tf_op jit(solution)/shard_map/ppermute | solution.py:570
  201.3 13.0 %collective-permute-start.20 = (bf16[1,4,48,768]{3,2,1,0:T(8,128)(2,1)S(1)}, bf16[1,4,48,768]{3,2,1,0:T(8,128)(2,1)S(1)}, u32[]{:S(2)}, u32[]{:S(2)}) collective-permute-start(bf16[1,4,48,768]{3,2,1,0:T(8,128)(2,1)S(1)} %get-tuple-element.166), channel_id=1, source_target_pairs={{0,4},{1,5},{2,6},{3,7},{4,0},{5,1},{6,2},{7,3},{8,12},{9,13},{10,... | collective-permute-start | bytes 884744 | tf_op jit(solution)/shard_map/ppermute | solution.py:570
  214.3 6.6 %collective-permute-start.24 = (bf16[2,48,768]{2,1,0:T(8,128)(2,1)S(1)}, bf16[2,48,768]{2,1,0:T(8,128)(2,1)S(1)}, u32[]{:S(2)}, u32[]{:S(2)}) collective-permute-start(bf16[2,48,768]{2,1,0:T(8,128)(2,1)S(1)} %get-tuple-element.174), channel_id=1, source_target_pairs={{0,48},{1,49},{2,50},{3,51},{4,52},{5,53},{6,54},{7,55},{8,56},{9,... | collective-permute-start | bytes 442376 | tf_op jit(solution)/shard_map/ppermute | solution.py:570
  214.9 7.6 %collective-permute-start.22 = (bf16[3,48,768]{2,1,0:T(8,128)(2,1)S(1)}, bf16[3,48,768]{2,1,0:T(8,128)(2,1)S(1)}, u32[]{:S(2)}, u32[]{:S(2)}) collective-permute-start(bf16[3,48,768]{2,1,0:T(8,128)(2,1)S(1)} %pad_maximum_fusion.10), channel_id=1, source_target_pairs={{0,12},{1,13},{2,14},{3,15},{4,8},{5,9},{6,10},{7,11},{8,4},{9,5},... | collective-permute-start | bytes 663560 | tf_op jit(solution)/shard_map/ppermute | solution.py:570
  221.0 4.5 %collective-permute-start.25 = (bf16[1,48,768]{2,1,0:T(8,128)(2,1)S(1)}, bf16[1,48,768]{2,1,0:T(8,128)(2,1)S(1)}, u32[]{:S(2)}, u32[]{:S(2)}) collective-permute-start(bf16[1,48,768]{2,1,0:T(8,128)(2,1)S(1)} %fusion.4), channel_id=1, source_target_pairs={{0,16},{1,17},{2,18},{3,19},{4,20},{5,21},{6,22},{7,23},{8,24},{9,... | collective-permute-start | bytes 221192 | tf_op jit(solution)/shard_map/ppermute | solution.py:570
  222.6 5.3 %collective-permute-start.23 = (bf16[2,48,768]{2,1,0:T(8,128)(2,1)S(1)}, bf16[2,48,768]{2,1,0:T(8,128)(2,1)S(1)}, u32[]{:S(2)}, u32[]{:S(2)}) collective-permute-start(bf16[2,48,768]{2,1,0:T(8,128)(2,1)S(1)} %pad_maximum_fusion.13), channel_id=1, source_target_pairs={{0,4},{1,5},{2,6},{3,7},{4,0},{5,1},{6,2},{7,3},{8,12},{9,13},{10,... | collective-permute-start | bytes 442376 | tf_op jit(solution)/shard_map/ppermute | solution.py:570
  228.1 6.3 %collective-permute-start.26 = (bf16[48,2304]{1,0:T(8,128)(2,1)S(1)}, bf16[48,2304]{1,0:T(8,128)(2,1)S(1)}, u32[]{:S(2)}, u32[]{:S(2)}) collective-permute-start(bf16[48,2304]{1,0:T(8,128)(2,1)S(1)} %fusion.13), channel_id=1, source_target_pairs={{0,1},{1,0},{2,3},{3,2},{4,5},{5,4},{6,7},{7,6},{8,9},{9,8},{10,11... | collective-permute-start | bytes 663560 | tf_op jit(solution)/shard_map/ppermute | solution.py:570
  230.3 12.0 %collective-permute-start.28 = (bf16[2,208,768]{2,1,0:T(8,128)(2,1)S(1)}, bf16[2,208,768]{2,1,0:T(8,128)(2,1)S(1)}, u32[]{:S(2)}, u32[]{:S(2)}) collective-permute-start(bf16[2,208,768]{2,1,0:T(8,128)(2,1)S(1)} %pad_maximum_fusion.2), channel_id=1, source_target_pairs={{0,3},{1,2},{2,1},{3,0},{4,7},{5,6},{6,5},{7,4},{8,11},{9,10},{10,... | collective-permute-start | bytes 1916936 | tf_op jit(solution)/shard_map/ppermute | solution.py:570
  234.4 10.3 %collective-permute-start.27 = (bf16[48,2304]{1,0:T(8,128)(2,1)S(1)}, bf16[48,2304]{1,0:T(8,128)(2,1)S(1)}, u32[]{:S(2)}, u32[]{:S(2)}) collective-permute-start(bf16[48,2304]{1,0:T(8,128)(2,1)S(1)} %add_convert_fusion.7), channel_id=1, source_target_pairs={{0,3},{1,2},{2,1},{3,0},{4,7},{5,6},{6,5},{7,4},{8,11},{9,10},{10,... | collective-permute-start | bytes 663560 | tf_op jit(solution)/shard_map/ppermute | solution.py:570
  249.0 11.7 %collective-permute-start.29 = (bf16[48,7680]{1,0:T(8,128)(2,1)}, bf16[48,7680]{1,0:T(8,128)(2,1)S(1)}, u32[]{:S(2)}, u32[]{:S(2)}) collective-permute-start(bf16[48,7680]{1,0:T(8,128)(2,1)} %reduce-scatter.2.cloned.1.call-done), channel_id=1, source_target_pairs={{0,1},{1,0},{2,3},{3,2},{4,5},{5,4},{6,7},{7,6},{8,9},{9,8},{10,11... | collective-permute-start | bytes 2211848 | tf_op jit(solution)/shard_map/ppermute | solution.py:570
  262.1 10.7 %collective-permute-start.30 = (bf16[48,7680]{1,0:T(8,128)(2,1)S(1)}, bf16[48,7680]{1,0:T(8,128)(2,1)S(1)}, u32[]{:S(2)}, u32[]{:S(2)}) collective-permute-start(bf16[48,7680]{1,0:T(8,128)(2,1)S(1)} %add_convert_fusion.1), channel_id=1, source_target_pairs={{0,3},{1,2},{2,1},{3,0},{4,7},{5,6},{6,5},{7,4},{8,11},{9,10},{10,... | collective-permute-start | bytes 2211848 | tf_op jit(solution)/shard_map/ppermute | solution.py:570
  273.1 4.5 %collective-permute-start.31 = (bf16[48,5376]{1,0:T(8,128)(2,1)S(1)}, bf16[48,5376]{1,0:T(8,128)(2,1)S(1)}, u32[]{:S(2)}, u32[]{:S(2)}) collective-permute-start(bf16[48,5376]{1,0:T(8,128)(2,1)S(1)} %broadcast_select_fusion.2), channel_id=1, source_target_pairs={{0,64},{64,0},{1,65},{65,1},{2,66},{66,2},{3,67},{67,3},{4,68},{68... | collective-permute-start | bytes 1548296 | tf_op jit(solution)/shard_map/ppermute | solution.py:557
  (35 other events, 288.3 us)
Sparse Core Ops, SparseCore 0:
  15.2 92.7 all-gather.3
  148.4 100.6 reduce-scatter.1
